TPU v7x, 512 devices: a whole 4x8x8 slice. The times are simulated.
512 devices in a mesh: dp: 32 (over y, x_lo, core), mp: 16 (over x_hi, z).
Axes of the slice: x: 4 (x_hi: 2, x_lo: 2; x = x_hi * 2 + x_lo), y: 8, z: 8, core: 2. Of those that a mesh axis runs over, the one named last changes fastest.
Arguments:
- tokens: bfloat16 [8192, 2560], P('dp', 'mp'), may hold values from -6 to 6
- cotangent: bfloat16 [8192, 2560], P('dp', 'mp'), may hold values from -130085.49 to 130085.49
- gate_weight: bfloat16 [2560, 6912], P('dp', 'mp'), may hold values from -0.125 to 0.125
- up_weight: bfloat16 [2560, 6912], P('dp', 'mp'), may hold values from -5.9885633 to 5.9885633
- probe_gate: bfloat16 [2560, 6912], P('dp', 'mp'), may hold values from -6 to 6
- probe_up: bfloat16 [2560, 6912], P('dp', 'mp'), may hold values from -6 to 6
- probe_down: bfloat16 [2560, 6912], P('dp', 'mp'), may hold values from -6 to 6
- moment: float32 [2560, 6912], P('dp', 'mp'), may hold values from -0.12 to 0.12
- curvature: float32 [2560, 6912], P('dp', 'mp'), may hold values from 0.2 to 2
- step_count: int32 [], replicated, may hold values from 1 to 63
Outputs:
- moment_next: float32 [2560, 6912], P('dp', 'mp')
- curvature_next: float32 [2560, 6912], P('dp', 'mp')
- direction: bfloat16 [2560, 6912], P('dp', 'mp')
Inputs may be any that keep to these rules, and one draw needn't show every extreme that they name: `step_count`: the number of optimizer steps taken, this one included, within the first steps after a restart.
All inputs are finite; a program needn't handle non-finite values.
Results may differ from a plain program's by a relative error of at most 0.04.
Values may be sent and summed in bfloat16 or wider, within the bound.
No kernel may reach another device: no remote copies, remote signals or barrier semaphores. Data moves between devices by JAX's collectives and lax.ppermute only.
A program may use at most 64 MiB of HBM per device.

v0:
```python
import math

import jax
import jax.numpy as jnp
from jax import lax
from jax.sharding import PartitionSpec as P

DW = 2560
FFW = 6912


CLIP_RMS = 0.5
GAMMA = 0.03
FLOOR = 0.01


def contract_tokens(left_rows, right_rows):
    return lax.dot_general(
        left_rows, right_rows, (((0,), (0,)), ((), ())), preferred_element_type=jnp.float32
    )


def swiglu_pair(gate_pre, up_pre, gate_dot, up_dot):
    sigmoid_val = jax.nn.sigmoid(gate_pre)
    silu_val = gate_pre * sigmoid_val
    silu_slope = sigmoid_val * (1.0 + gate_pre * (1.0 - sigmoid_val))
    hidden = (silu_val * up_pre).astype(jnp.bfloat16)
    hidden_dot = (silu_slope * up_pre * gate_dot + silu_val * up_dot).astype(jnp.bfloat16)
    return (hidden, hidden_dot)


def per_device(
    tokens,
    cotangent,
    gate_weight,
    up_weight,
    probe_gate,
    probe_up,
    probe_down,
    moment,
    curvature,
    step_count,
):
    gathered_tokens, gathered_cot = (
        lax.all_gather(tokens, "mp", axis=1, tiled=True),
        lax.all_gather(cotangent, "mp", axis=1, tiled=True),
    )
    token_rows = gathered_tokens.shape[0]
    shard_rows = gate_weight.shape[0]
    local_units = gate_weight.shape[1]
    data_size = lax.axis_size("dp")
    total_tokens = token_rows * data_size

    def project_rows(pieces):
        return tuple(
            (
                jnp.dot(gathered_tokens, weight_piece, preferred_element_type=jnp.float32)
                for weight_piece in pieces
            )
        )

    gate_pre, up_pre = project_rows(
        (
            lax.all_gather(gate_weight, "dp", axis=0, tiled=True),
            lax.all_gather(up_weight, "dp", axis=0, tiled=True),
        )
    )
    gate_dot, up_dot = project_rows(
        (
            lax.all_gather(probe_gate, "dp", axis=0, tiled=True),
            lax.all_gather(probe_up, "dp", axis=0, tiled=True),
        )
    )
    hidden, hidden_dot = swiglu_pair(gate_pre, up_pre, gate_dot, up_dot)
    curv_term = (contract_tokens(gathered_cot, hidden_dot) / total_tokens).astype(jnp.bfloat16)
    curv_term = curv_term.reshape(data_size, shard_rows, local_units)
    gradient = lax.psum_scatter(
        (contract_tokens(gathered_cot, hidden) / total_tokens).astype(jnp.bfloat16),
        "dp",
        scatter_dimension=0,
        tiled=True,
    ).astype(jnp.float32)
    curv_parts = lax.all_to_all(curv_term, "dp", split_axis=0, concat_axis=0, tiled=True)
    hess_vec = jnp.sum(curv_parts.astype(jnp.float32), axis=0)
    norm_total = lax.psum(jnp.sum(gradient * gradient), ("dp", "mp"))
    factor = jnp.minimum(1.0, CLIP_RMS * math.sqrt(DW * FFW) / (jnp.sqrt(norm_total) + 1e-06))
    moment_next = 0.96 * moment + 0.04 * (factor * gradient)
    curvature_next = 0.99 * curvature + 0.01 * (probe_down.astype(jnp.float32) * hess_vec)
    step_float = step_count.astype(jnp.float32)
    first_fix = 1.0 - jnp.power(jnp.float32(0.96), step_float)
    second_fix = 1.0 - jnp.power(jnp.float32(0.99), step_float)
    ratio = moment_next / first_fix / jnp.maximum(GAMMA * curvature_next / second_fix, FLOOR)
    direction = jnp.clip(ratio, -1.0, 1.0).astype(jnp.bfloat16)
    return (moment_next, curvature_next, direction)


def solution(mesh):
    placed = (
        P("dp", "mp"),
        P("dp", "mp"),
        P("dp", "mp"),
        P("dp", "mp"),
        P("dp", "mp"),
        P("dp", "mp"),
        P("dp", "mp"),
        P("dp", "mp"),
        P("dp", "mp"),
        P(),
    )
    return jax.shard_map(
        per_device,
        mesh=mesh,
        in_specs=placed,
        out_specs=(P("dp", "mp"), P("dp", "mp"), P("dp", "mp")),
        check_vma=False,
    )
```

profile of v0, /device:TPU:1, one launch (start us, length us, event | category | flops | bytes accessed | tf_op | source)
XLA Modules:
  0.0 719.6 jit_solution(9656301686221109859)
XLA Ops:
  7.2 0.0 all-gather.7.cloned.1.call-start
  7.2 0.7 all-gather.7.cloned.1.call-update
  7.9 0.0 all-gather.9.cloned.1.call-start
  7.9 0.7 all-gather.9.cloned.1.call-update
  8.6 0.0 all-gather.11.cloned.1.call-start
  8.7 0.7 all-gather.11.cloned.1.call-update
  9.4 0.0 all-gather.13.cloned.1.call-start
  9.4 0.5 all-gather.13.cloned.1.call-update
  10.0 0.0 all-gather.17.cloned.1.call-start
  10.0 0.5 all-gather.17.cloned.1.call-update
  10.5 0.0 all-gather.15.cloned.1.call-start
  10.6 0.5 all-gather.15.cloned.1.call-update
  11.1 0.0 reduce-scatter.4.cloned.1.call-start
  11.2 88.7 %all-gather.7.cloned.1.call-done = bf16[256,2560]{0,1:T(8,128)(2,1)} async-done(((bf16[256,160]{0,1:T(8,128)(2,1)}), bf16[256,2560]{0,1:T(8,128)(2,1)}) %all-gather.7.cloned.1.call-update) | async-done | bytes 1310736 | tf_op jit(solution)/shard_map/all_gather | solution.py:45
  99.9 70.4 %all-gather.9.cloned.1.call-done = bf16[2560,432]{1,0:T(8,128)(2,1)} async-done(((bf16[80,432]{1,0:T(8,128)(2,1)}), bf16[2560,432]{1,0:T(8,128)(2,1)}) %all-gather.9.cloned.1.call-update) | async-done | bytes 2211856 | tf_op jit(solution)/shard_map/all_gather | solution.py:64
  170.3 4.0 fusion.20
  174.3 66.2 %all-gather.11.cloned.1.call-done = bf16[2560,432]{1,0:T(8,128)(2,1)} async-done(((bf16[80,432]{1,0:T(8,128)(2,1)}), bf16[2560,432]{1,0:T(8,128)(2,1)}) %all-gather.11.cloned.1.call-update) | async-done | bytes 2211856 | tf_op jit(solution)/shard_map/all_gather | solution.py:65
  240.5 3.6 fusion.21
  244.1 82.3 %all-gather.13.cloned.1.call-done = bf16[256,2560]{0,1:T(8,128)(2,1)} async-done(((bf16[256,160]{0,1:T(8,128)(2,1)}), bf16[256,2560]{0,1:T(8,128)(2,1)}) %all-gather.13.cloned.1.call-update) | async-done | bytes 1310736 | tf_op jit(solution)/shard_map/all_gather | solution.py:46
  326.3 2.4 fusion.3
  328.7 2.6 copy.28
  331.4 65.2 %all-gather.17.cloned.1.call-done = bf16[2560,432]{1,0:T(8,128)(2,1)} async-done(((bf16[80,432]{1,0:T(8,128)(2,1)}), bf16[2560,432]{1,0:T(8,128)(2,1)}) %all-gather.17.cloned.1.call-update) | async-done | bytes 2211856 | tf_op jit(solution)/shard_map/all_gather | solution.py:71
  396.6 3.6 convolution_multiply_fusion.2
  400.2 66.4 %all-gather.15.cloned.1.call-done = bf16[2560,432]{1,0:T(8,128)(2,1)} async-done(((bf16[80,432]{1,0:T(8,128)(2,1)}), bf16[2560,432]{1,0:T(8,128)(2,1)}) %all-gather.15.cloned.1.call-update) | async-done | bytes 2211856 | tf_op jit(solution)/shard_map/all_gather | solution.py:70
  466.7 5.0 fusion.2
  471.7 2.6 copy.27
  474.3 6.5 all-to-all-start
  481.6 128.7 %reduce-scatter.4.cloned.1.call-done = bf16[80,432]{1,0:T(8,128)(2,1)} async-done(((bf16[2560,432]{1,0:T(8,128)(2,1)}), bf16[80,432]{1,0:T(8,128)(2,1)}) %reduce-scatter.4.cloned.1.call-update) | async-done | bytes 69136 | tf_op jit(solution)/shard_map/reduce_scatter | solution.py:77
  610.4 1.6 fusion.13
  612.0 0.4 convert_reduce_fusion
  612.4 98.8 %psum.7 = f32[]{:T(128)} all-reduce(f32[]{:T(128)} %fusion.13), channel_id=1, replica_groups=mesh['dp'=32,'mp'=16] {'dp','mp'}, use_global_device_ids=true, to_apply=%region_2.0 | all-reduce | flops 1 | bytes 8 | tf_op jit(solution)/shard_map/psum | solution.py:85
  712.0 0.8 clamp_convert_fusion
  (14 shorter events, 0.0 us)
Async XLA Ops:
  7.2 92.7 %all-gather.7.cloned.1.call-start = ((), (), s32[]{:S(2)}) async-start(), calls=%async_computation.2 | async-start | bytes 1392640 | tf_op jit(solution)/shard_map/all_gather | solution.py:45
  7.9 162.4 %all-gather.9.cloned.1.call-start = ((), (), s32[]{:S(2)}) async-start(), calls=%async_computation.3 | async-start | bytes 2703360 | tf_op jit(solution)/shard_map/all_gather | solution.py:64
  8.6 231.8 %all-gather.11.cloned.1.call-start = ((), (), s32[]{:S(2)}) async-start(), calls=%async_computation.4 | async-start | bytes 2703360 | tf_op jit(solution)/shard_map/all_gather | solution.py:65
  9.4 317.0 %all-gather.13.cloned.1.call-start = ((), (), s32[]{:S(2)}) async-start(), calls=%async_computation.5 | async-start | bytes 1392640 | tf_op jit(solution)/shard_map/all_gather | solution.py:46
  10.0 386.6 %all-gather.17.cloned.1.call-start = ((), (), s32[]{:S(2)}) async-start(), calls=%async_computation.7 | async-start | bytes 2703360 | tf_op jit(solution)/shard_map/all_gather | solution.py:71
  10.5 456.1 %all-gather.15.cloned.1.call-start = ((), (), s32[]{:S(2)}) async-start(), calls=%async_computation.6 | async-start | bytes 2703360 | tf_op jit(solution)/shard_map/all_gather | solution.py:70
  11.1 599.2 %reduce-scatter.4.cloned.1.call-start = ((), (), s32[]{:S(2)}) async-start(), calls=%async_computation.8 | async-start | bytes 2703360 | tf_op jit(solution)/shard_map/reduce_scatter | solution.py:77
  99.9 140.6 %copy-start = (bf16[256,2560]{0,1:T(8,128)(2,1)S(1)}, bf16[256,2560]{0,1:T(8,128)(2,1)}, u32[]{:S(2)}) copy-start(bf16[256,2560]{0,1:T(8,128)(2,1)} %all-gather.7.cloned.1.call-done) | copy-start | bytes 3932164
  331.3 65.2 %copy-start.1 = (f32[256,432]{0,1:T(8,128)S(1)}, f32[256,432]{0,1:T(8,128)}, u32[]{:S(2)}) copy-start(f32[256,432]{0,1:T(8,128)} %fusion.20) | copy-start | bytes 1327108
  474.3 137.7 %all-to-all-start = ((bf16[32,80,432]{2,1,0:T(8,128)(2,1)}), bf16[32,80,432]{2,1,0:T(8,128)(2,1)S(1)}, u32[]{:S(2)}, u32[]{:S(2)}) async-start(bf16[32,80,432]{2,1,0:T(8,128)(2,1)} %bitcast.16), calls=%async_computation | async-start | bytes 5242880 | tf_op jit(solution)/shard_map/all_to_all | solution.py:83
  480.8 231.2 %copy-start.3 = (f32[80,432]{1,0:T(8,128)S(1)}, f32[80,432]{1,0:T(8,128)}, u32[]{:S(2)}) copy-start(f32[80,432]{1,0:T(8,128)} %param.18) | copy-start | bytes 414724
  480.8 231.2 %copy-start.4 = (f32[80,432]{1,0:T(8,128)S(1)}, f32[80,432]{1,0:T(8,128)}, u32[]{:S(2)}) copy-start(f32[80,432]{1,0:T(8,128)} %param.17) | copy-start | bytes 414724
  480.8 231.2 %copy-start.5 = (bf16[80,432]{1,0:T(8,128)(2,1)S(1)}, bf16[80,432]{1,0:T(8,128)(2,1)}, u32[]{:S(2)}) copy-start(bf16[80,432]{1,0:T(8,128)(2,1)} %param.16) | copy-start | bytes 207364
  610.4 101.6 %copy-start.2 = (bf16[80,432]{1,0:T(8,128)(2,1)S(1)}, bf16[80,432]{1,0:T(8,128)(2,1)}, u32[]{:S(2)}) copy-start(bf16[80,432]{1,0:T(8,128)(2,1)} %reduce-scatter.4.cloned.1.call-done) | copy-start | bytes 207364
Sparse Core Ops, SparseCore 0:
  11.2 88.6 all-gather.6
  102.0 68.2 all-gather.8
  172.4 68.0 all-gather.10
  243.5 82.7 all-gather.12
  328.3 68.2 all-gather.16
  398.6 68.0 all-gather.14
  469.5 140.8 reduce-scatter.3
where the time goes:
time: 720 us
  waiting for transfers between devices  572 us (79%)
  blocking collectives  98.8 us (14%)
  matrix products  18.6 us (3%)
  between operations  15.7 us (2%)
    reduce_scatter x1, waiting for transfers between devices, per_device(): lax.psum_scatter((contract_tokens(gathered_cot, hidden) / total_tokens).a...  129 us
    psum x1, blocking collectives, per_device(): norm_total = lax.psum(jnp.sum(gradient * gradient), ('dp', 'mp'))  98.8 us
    all_gather x1, waiting for transfers between devices, per_device(): lax.all_gather(tokens, 'mp', axis=1, tiled=True)  88.7 us
    all_gather x1, waiting for transfers between devices, per_device(): lax.all_gather(cotangent, 'mp', axis=1, tiled=True)  82.3 us
    all_gather x1, waiting for transfers between devices, per_device(): lax.all_gather(gate_weight, 'dp', axis=0, tiled=True)  70.4 us
    all_gather x1, waiting for transfers between devices, per_device(): lax.all_gather(probe_gate, 'dp', axis=0, tiled=True)  66.4 us
    all_gather x1, waiting for transfers between devices, per_device(): lax.all_gather(up_weight, 'dp', axis=0, tiled=True)  66.2 us
    all_gather x1, waiting for transfers between devices, per_device(): lax.all_gather(probe_up, 'dp', axis=0, tiled=True)  65.2 us
  transfers between devices with their start and end apart: 8, of which 7 were waited for; matrix products, arithmetic and copies ran while one was open for 4% of the time, Pallas kernels for 0%

commit v1 on v0

v1 whole, which is shorter than its diff:
```python
import functools
import math

import jax
import jax.numpy as jnp
from jax import lax
from jax.experimental import pallas as pl
from jax.experimental.pallas import tpu as pltpu
from jax.sharding import Mesh, PartitionSpec as P

DW = 2560
FFW = 6912
TOKENS = 8192

CLIP_RMS = 0.5
GAMMA = 0.03
FLOOR = 0.01

SIZES = (8, 2, 2, 2, 8)
NAMES = ("y", "xl", "core", "xh", "z")
DP = ("y", "xl", "core")
CHIPS = ("y", "xl")
MP = ("xh", "z")

COLUMNS = 256
FORWARD_VMEM = 54 * 1024 * 1024
BACKWARD_VMEM = 16 * 1024 * 1024


def forward_kernel(feat_ref, w_ref, out_ref, tok_ref):
    lines, planes, depth, rows = feat_ref.shape
    half = lines // 2

    @pl.when(pl.program_id(0) == 0)
    def _():
        for part in range(2 * planes):
            first = half * (part % 2)
            piece = feat_ref[first : first + half, part // 2].reshape(half * depth, rows)
            tok_ref[:, part * half * depth : (part + 1) * half * depth] = piece.T

    def project(which):
        piece = w_ref[:, which].reshape(tok_ref.shape[1], w_ref.shape[3])
        return jnp.dot(tok_ref[...], piece, preferred_element_type=jnp.float32)

    gate_pre, up_pre, gate_dot, up_dot = (project(which) for which in range(4))
    sigmoid_val = jax.nn.sigmoid(gate_pre)
    silu_val = gate_pre * sigmoid_val
    silu_slope = sigmoid_val * (1.0 + gate_pre * (1.0 - sigmoid_val))
    out_ref[0] = (silu_val * up_pre).astype(jnp.bfloat16)
    out_ref[1] = (silu_slope * up_pre * gate_dot + silu_val * up_dot).astype(jnp.bfloat16)


def forward(features, weights):
    lines, planes, double, rows = features.shape
    shards, _, depth, units = weights.shape
    width = double // 2
    inputs = lines * planes * width
    return pl.pallas_call(
        forward_kernel,
        out_shape=jax.ShapeDtypeStruct((2, rows, units), jnp.bfloat16),
        grid=(pl.cdiv(units, COLUMNS),),
        in_specs=[
            pl.BlockSpec((lines, planes, width, rows), lambda j: (0, 0, 0, 0)),
            pl.BlockSpec((shards, 4, depth, COLUMNS), lambda j: (0, 0, 0, j)),
        ],
        out_specs=pl.BlockSpec((2, rows, COLUMNS), lambda j: (0, 0, j)),
        scratch_shapes=[pltpu.VMEM((rows, inputs), jnp.bfloat16)],
        compiler_params=pltpu.CompilerParams(vmem_limit_bytes=FORWARD_VMEM),
        cost_estimate=pl.CostEstimate(
            flops=2 * rows * inputs * 4 * units,
            bytes_accessed=weights.size * 2 + inputs * rows * 2,
            transcendentals=rows * units,
        ),
    )(features, weights)


def top_column(block):
    size = jnp.max(jnp.abs(block), axis=0, keepdims=True)
    lane = lax.broadcasted_iota(jnp.int32, size.shape, 1)
    first = jnp.where(size == jnp.max(size, axis=1, keepdims=True), lane, size.shape[1])
    return lane == jnp.min(first, axis=1, keepdims=True)


def rounded_with_rest(block):
    high = block.astype(jnp.bfloat16).astype(jnp.float32)
    rest = jnp.where(top_column(high), block - high, 0.0)
    return high, jnp.sum(rest, axis=1, keepdims=True)


def backward_kernel(cot_ref, mine_ref, other_ref, out_ref):
    blocks, _, double, rows = cot_ref.shape
    depth = double // 2
    sides = []
    for which in range(2):
        piece = cot_ref[:, 0, which * depth : (which + 1) * depth]
        sides.append(piece.reshape(blocks * depth, rows))

    def summed(kind):
        total = 0.0
        for cot, ref in zip(sides, (mine_ref, other_ref)):
            partial = jnp.dot(cot, ref[kind], preferred_element_type=jnp.float32) * (1.0 / TOKENS)
            total += partial.astype(jnp.bfloat16).astype(jnp.float32)
        return total

    totals = [summed(kind) for kind in range(2)]
    for index in range(blocks):
        parts = []
        for total in totals:
            parts += rounded_with_rest(total[index * depth : (index + 1) * depth])
        out_ref[index] = jnp.concatenate(parts, axis=1).astype(jnp.bfloat16)


def backward(features, mine, other):
    lines, planes, double, rows = features.shape
    units = mine.shape[2]
    depth = double // 4
    shards = lines * planes
    parts = 4
    block = shards // parts
    per_plane = parts // planes
    return pl.pallas_call(
        backward_kernel,
        out_shape=jax.ShapeDtypeStruct((shards, depth, 2 * units + 2), jnp.bfloat16),
        grid=(parts,),
        in_specs=[
            pl.BlockSpec(
                (block, 1, double // 2, rows), lambda i: (i % per_plane, i // per_plane, 1, 0)
            ),
            pl.BlockSpec(mine.shape, lambda i: (0, 0, 0)),
            pl.BlockSpec(mine.shape, lambda i: (0, 0, 0)),
        ],
        out_specs=pl.BlockSpec((block, depth, 2 * units + 2), lambda i: (i, 0, 0)),
        compiler_params=pltpu.CompilerParams(vmem_limit_bytes=BACKWARD_VMEM),
        cost_estimate=pl.CostEstimate(
            flops=2 * shards * depth * 4 * rows * units,
            bytes_accessed=2 * (features.size // 2 + 2 * mine.size + shards * depth * 2 * units),
            transcendentals=0,
        ),
    )(features, mine, other)


def gradient_kernel(packed_ref, gradient_ref, square_ref):
    units = gradient_ref.shape[1]
    total = jnp.zeros(gradient_ref.shape, jnp.float32)
    for index in range(packed_ref.shape[0]):
        block = packed_ref[index].astype(jnp.float32)
        high, rest = block[:, :units], block[:, units : units + 1]
        total += high + jnp.where(top_column(high), rest, 0.0)
    gradient_ref[...] = total
    square_ref[...] = jnp.full(square_ref.shape, jnp.sum(total * total))


def gradient_sum(packed, units):
    return pl.pallas_call(
        gradient_kernel,
        out_shape=(
            jax.ShapeDtypeStruct((packed.shape[1], units), jnp.float32),
            jax.ShapeDtypeStruct((1, 128), jnp.float32),
        ),
        compiler_params=pltpu.CompilerParams(vmem_limit_bytes=BACKWARD_VMEM),
    )(packed)


def hessian_kernel(packed_ref, out_ref):
    units = out_ref.shape[1]
    total = jnp.zeros(out_ref.shape, jnp.float32)
    for index in range(packed_ref.shape[0]):
        block = packed_ref[index].astype(jnp.float32)
        high, rest = block[:, units + 1 : 2 * units + 1], block[:, 2 * units + 1 :]
        total += high + jnp.where(top_column(high), rest, 0.0)
    out_ref[...] = total


def hessian_sum(packed, units):
    return pl.pallas_call(
        hessian_kernel,
        out_shape=jax.ShapeDtypeStruct((packed.shape[1], units), jnp.float32),
        compiler_params=pltpu.CompilerParams(vmem_limit_bytes=BACKWARD_VMEM),
    )(packed)


def swap_cores(value):
    return lax.ppermute(value, "core", [(0, 1), (1, 0)])


def to_all(value, axes):
    copies = jnp.broadcast_to(value[None], (lax.axis_size(axes),) + value.shape)
    return lax.all_to_all(copies, axes, 0, 0, tiled=True)


def gather_features(value):
    other = lax.ppermute(value, "xh", [(0, 1), (1, 0)])
    low = lax.axis_index("xh") == 0
    pair = jnp.stack([jnp.where(low, value, other), jnp.where(low, other, value)])
    return to_all(pair, "z")


def sum_over_all(square):
    for axes in (MP, DP):
        square = jnp.sum(to_all(square, axes), axis=0)
    return square[0, 0]


def per_device(
    tokens,
    cotangent,
    gate_weight,
    up_weight,
    probe_gate,
    probe_up,
    probe_down,
    moment,
    curvature,
    step_count,
):
    core = lax.axis_index("core")
    shard_rows, units = gate_weight.shape

    weights = lax.all_gather(
        jnp.stack([gate_weight, up_weight, probe_gate, probe_up]), DP, axis=0, tiled=False
    )
    cot_t = cotangent.T
    cot_mine = lax.dynamic_slice_in_dim(cot_t, core * shard_rows, shard_rows, 0)
    cot_send = lax.dynamic_slice_in_dim(cot_t, (1 - core) * shard_rows, shard_rows, 0)
    features = gather_features(jnp.concatenate([tokens.T, cot_mine, swap_cores(cot_send)]))
    weights, features = lax.optimization_barrier((weights, features))

    hidden = forward(features, weights)
    packed = backward(features, hidden, swap_cores(hidden))
    packed = lax.all_to_all(packed, CHIPS, 0, 0, tiled=True)
    gradient, square = gradient_sum(packed, units)
    norm_total = sum_over_all(square)
    hess_vec = hessian_sum(packed, units)

    factor = jnp.minimum(1.0, CLIP_RMS * math.sqrt(DW * FFW) / (jnp.sqrt(norm_total) + 1e-06))
    moment_next = 0.96 * moment + 0.04 * (factor * gradient)
    curvature_next = 0.99 * curvature + 0.01 * (probe_down.astype(jnp.float32) * hess_vec)
    step_float = step_count.astype(jnp.float32)
    first_fix = 1.0 - jnp.power(jnp.float32(0.96), step_float)
    second_fix = 1.0 - jnp.power(jnp.float32(0.99), step_float)
    ratio = moment_next / first_fix / jnp.maximum(GAMMA * curvature_next / second_fix, FLOOR)
    direction = jnp.clip(ratio, -1.0, 1.0).astype(jnp.bfloat16)
    return (moment_next, curvature_next, direction)


def solution(mesh):
    fine = Mesh(mesh.devices.reshape(SIZES), NAMES)
    block = P(DP, MP)
    return jax.shard_map(
        per_device,
        mesh=fine,
        in_specs=(block,) * 9 + (P(),),
        out_specs=(block,) * 3,
        check_vma=False,
    )
```

time: 720 us -> 215 us (0.30)
  waiting for transfers between devices: 572 us -> 13.1 us
  blocking collectives: 98.8 us -> 140 us
  matrix products: 18.6 us -> 0 us
  Pallas kernels: 0 us -> 16.5 us
  starting transfers between devices: 6.79 us -> 22.7 us
    all_gather x6 -> x1, waiting for transfers between devices: 439 us -> 0.01 us  [per_device(): lax.all_gather(jnp.stack([gate_weight, up_weight, probe_gate, probe_up]),...]
    all_to_all x0 -> x3, blocking collectives: none -> 140 us  [the longest x2 77.3 us: to_all(): return lax.all_to_all(copies, axes, 0, 0, tiled=True)]
    reduce_scatter x1 -> x0, waiting for transfers between devices: 129 us -> none  [per_device(): lax.psum_scatter((contract_tokens(gathered_cot, hidden) / total_tokens).a...]
    psum x1 -> x0, blocking collectives: 98.8 us -> none  [per_device(): norm_total = lax.psum(jnp.sum(gradient * gradient), ('dp', 'mp'))]
    dot_general x5 -> x0, matrix products: 18.6 us -> none  [the longest x3 11.3 us: project_rows(): jnp.dot(gathered_tokens, weight_piece, preferred_element_type=jnp.float32)]
    pallas_call x0 -> x4, Pallas kernels: none -> 16.5 us  [the longest x1 7.23 us: forward(): pl.pallas_call(forward_kernel, out_shape=jax.ShapeDtypeStruct((2, rows, u...]
    ppermute x0 -> x3, starting transfers between devices: none -> 15.7 us  [the longest x2 13.8 us: swap_cores(): return lax.ppermute(value, 'core', [(0, 1), (1, 0)])]
    ppermute x0 -> x3, waiting for transfers between devices: none -> 9.47 us  [the longest x1 6.9 us: gather_features(): other = lax.ppermute(value, 'xh', [(0, 1), (1, 0)])]
  transfers between devices with their start and end apart: 8 -> 5, of which waited for: 7 -> 4; matrix products, arithmetic and copies ran while one was open for 4% -> 1% of each run, Pallas kernels for 0% -> 2%
where the time goes in v1:
time: 215 us; the launch traced here: 214 us
  blocking collectives  140 us (65%)
  starting transfers between devices  22.7 us (11%)
  Pallas kernels  16.5 us (8%)
  between operations  15 us (7%)
  waiting for transfers between devices  13.1 us (6%)
  other arithmetic  4.5 us (2%)
  local copies, waits for them, and re-layouts  2.74 us (1%)
    all_to_all x2, blocking collectives, to_all(): return lax.all_to_all(copies, axes, 0, 0, tiled=True)  77.3 us
    all_to_all x1, blocking collectives, per_device(): packed = lax.all_to_all(packed, CHIPS, 0, 0, tiled=True)  62.4 us
    ppermute x2, starting transfers between devices, swap_cores(): return lax.ppermute(value, 'core', [(0, 1), (1, 0)])  13.8 us
    pallas_call x1, Pallas kernels, forward(): pl.pallas_call(forward_kernel, out_shape=jax.ShapeDtypeStruct((2, rows, u...  7.23 us
    all_to_all x1, starting transfers between devices, to_all(): return lax.all_to_all(copies, axes, 0, 0, tiled=True)  6.98 us
    ppermute x1, waiting for transfers between devices, gather_features(): other = lax.ppermute(value, 'xh', [(0, 1), (1, 0)])  6.9 us
    pallas_call x1, Pallas kernels, backward(): pl.pallas_call(backward_kernel, out_shape=jax.ShapeDtypeStruct((shards, d...  4.64 us
  transfers between devices with their start and end apart: 5, of which 4 were waited for; matrix products, arithmetic and copies ran while one was open for 1% of the time, Pallas kernels for 2%

profile of v1, /device:TPU:1, one launch (start us, length us, event | category | flops | bytes accessed | tf_op | source)
XLA Modules:
  0.0 214.3 jit_solution(10094806996142583698)
XLA Ops:
  7.2 0.0 all-gather.3.cloned.1.call-start
  7.2 1.8 pad_maximum_fusion
  9.0 0.0 all-gather.3.cloned.1.call-update
  9.0 0.8 dynamic-slice_bitcast_fusion.1
  9.8 8.8 %collective-permute-start = (bf16[80,256]{1,0:T(8,128)(2,1)S(1)}, bf16[80,256]{1,0:T(8,128)(2,1)S(1)}, u32[]{:S(2)}, u32[]{:S(2)}) collective-permute-start(bf16[80,256]{1,0:T(8,128)(2,1)S(1)} %get-tuple-element.17), channel_id=1, source_target_pairs={{0,16},{16,0},{1,17},{17,1},{2,18},{18,2},{3,19},{19,3},{4,20},{20... | collective-permute-start | bytes 122888 | tf_op jit(solution)/shard_map/ppermute | solution.py:183
  18.6 0.8 collective-permute-done
  19.5 0.9 pad_maximum_fusion.2
  20.4 1.9 collective-permute-start.1
  22.3 6.9 %collective-permute-done.1 = bf16[320,256]{1,0:T(8,128)(2,1)S(1)} collective-permute-done((bf16[320,256]{1,0:T(8,128)(2,1)S(1)}, bf16[320,256]{1,0:T(8,128)(2,1)S(1)}, u32[]{:S(2)}, u32[]{:S(2)}) %collective-permute-start.1) | collective-permute-done | bytes 163872 | tf_op jit(solution)/shard_map/ppermute | solution.py:192
  29.2 0.9 select_bitcast_fusion.1
  30.2 0.2 broadcast_in_dim.8
  30.5 64.8 %all_to_all.20.feat_ref.cot_ref = bf16[8,2,320,256]{3,2,1,0:T(8,128)(2,1)} all-to-all(bf16[8,2,320,256]{3,2,1,0:T(8,128)(2,1)S(1)} %broadcast_in_dim.8), channel_id=1, replica_groups=mesh['y'=8,'xl'=2,'core'=2,'xh'=2,'z'=8] {'z'}, dimensions={0} | all-to-all | bytes 5242880 | tf_op jit(solution)/shard_map/all_to_all | solution.py:188
  95.3 0.0 all-gather.3.cloned.1.call-done
  95.3 0.0 copy-start
  95.3 7.2 %shard_map.121.mine_ref = bf16[2,256,432]{2,1,0:T(8,128)(2,1)} custom-call(bf16[8,2,320,256]{3,2,1,0:T(8,128)(2,1)} %all_to_all.20.feat_ref.cot_ref, bf16[32,4,80,432]{3,2,1,0:T(8,128)(2,1)} %bitcast.21), custom_call_target="tpu_custom_call" | custom-call | flops 2264924160 | bytes 10158080 | tf_op jit(solution)/shard_map/pallas_call | solution.py:58
  102.5 5.0 %collective-permute-start.2 = (bf16[2,256,432]{2,1,0:T(8,128)(2,1)}, bf16[2,256,432]{2,1,0:T(8,128)(2,1)S(1)}, u32[]{:S(2)}, u32[]{:S(2)}) collective-permute-start(bf16[2,256,432]{2,1,0:T(8,128)(2,1)} %shard_map.121.mine_ref), channel_id=1, source_target_pairs={{0,16},{16,0},{1,17},{17,1},{2,18},{18,2},{3,19},{19,3},{4,20},{20... | collective-permute-start | bytes 1327112 | tf_op jit(solution)/shard_map/ppermute | solution.py:183
  107.6 1.7 collective-permute-done.2.other_ref
  109.3 0.0 copy-done
  109.3 0.0 copy-start.1
  109.3 1.0 copy-done.1
  110.3 4.6 %shard_map.122 = bf16[16,80,866]{2,1,0:T(8,128)(2,1)S(1)} custom-call(bf16[8,2,320,256]{3,2,1,0:T(8,128)(2,1)S(1)} %copy-done, bf16[2,256,432]{2,1,0:T(8,128)(2,1)S(1)} %copy-done.1, bf16[2,256,432]{2,1,0:T(8,128)(2,1)S(1)} %collective-permute-done.2.other_ref), custom_call_target="tpu_custom_call" | custom-call | flops 1132462080 | bytes 4407296 | tf_op jit(solution)/shard_map/pallas_call | solution.py:121
  115.0 62.4 %all_to_all.21.packed_ref = bf16[16,80,866]{2,1,0:T(8,128)(2,1)S(1)} all-to-all(bf16[16,80,866]{2,1,0:T(8,128)(2,1)S(1)} %shard_map.122), channel_id=1, replica_groups=mesh['y'=8,'xl'=2,'core'=2,'xh'=2,'z'=8] {'y','xl'}, dimensions={0} | all-to-all | bytes 4433920 | tf_op jit(solution)/shard_map/all_to_all | solution.py:230
  177.3 1.1 shard_map.123
  178.5 12.4 %all_to_all.22 = f32[16,1,128]{2,1,0:T(1,128)S(1)} all-to-all(f32[16,1,128]{2,1,0:T(1,128)S(1)} %broadcast_in_dim.10), channel_id=1, replica_groups=mesh['y'=8,'xl'=2,'core'=2,'xh'=2,'z'=8] {'xh','z'}, dimensions={0} | all-to-all | bytes 16384 | tf_op jit(solution)/shard_map/all_to_all | solution.py:188
  190.9 0.6 broadcast_in_dim.11
  191.5 7.0 %all-to-all-start.3 = ((f32[32,1,128]{2,1,0:T(1,128)}), f32[32,1,128]{2,1,0:T(1,128)S(1)}, u32[]{:S(2)}, u32[]{:S(2)}) async-start(f32[32,1,128]{2,1,0:T(1,128)} %broadcast_in_dim.11), calls=%async_computation.3 | async-start | bytes 32768 | tf_op jit(solution)/shard_map/all_to_all | solution.py:188
  199.3 3.6 %shard_map.124 = f32[80,432]{1,0:T(8,128)S(1)} custom-call(bf16[16,80,866]{2,1,0:T(8,128)(2,1)S(1)} %all_to_all.21.packed_ref), custom_call_target="tpu_custom_call" | custom-call | tf_op jit(solution)/shard_map/pallas_call | solution.py:175
  202.8 3.6 %all-to-all-done.3 = f32[32,1,128]{2,1,0:T(1,128)S(1)} async-done(((f32[32,1,128]{2,1,0:T(1,128)}), f32[32,1,128]{2,1,0:T(1,128)S(1)}, u32[]{:S(2)}, u32[]{:S(2)}) %all-to-all-start.3) | async-done | bytes 16416 | tf_op jit(solution)/shard_map/all_to_all | solution.py:188
  206.6 0.0 copy-done.2
  206.6 0.0 copy-done.3
  206.6 0.0 copy-done.4
  206.6 0.8 clamp_convert_fusion
  (7 shorter events, 0.1 us)
Async XLA Ops:
  7.2 88.1 %all-gather.3.cloned.1.call-start = ((), (), s32[]{:S(2)}) async-start(), calls=%async_computation.4 | async-start | bytes 10813440 | tf_op jit(solution)/shard_map/all_gather | solution.py:219
  9.8 9.6 %collective-permute-start = (bf16[80,256]{1,0:T(8,128)(2,1)S(1)}, bf16[80,256]{1,0:T(8,128)(2,1)S(1)}, u32[]{:S(2)}, u32[]{:S(2)}) collective-permute-start(bf16[80,256]{1,0:T(8,128)(2,1)S(1)} %get-tuple-element.17), channel_id=1, source_target_pairs={{0,16},{16,0},{1,17},{17,1},{2,18},{18,2},{3,19},{19,3},{4,20},{20... | collective-permute-start | bytes 122888 | tf_op jit(solution)/shard_map/ppermute | solution.py:183
  20.4 8.8 %collective-permute-start.1 = (bf16[320,256]{1,0:T(8,128)(2,1)S(1)}, bf16[320,256]{1,0:T(8,128)(2,1)S(1)}, u32[]{:S(2)}, u32[]{:S(2)}) collective-permute-start(bf16[320,256]{1,0:T(8,128)(2,1)S(1)} %pad_maximum_fusion.2), channel_id=1, source_target_pairs={{0,8},{8,0},{1,9},{9,1},{2,10},{10,2},{3,11},{11,3},{4,12},{12,4},... | collective-permute-start | bytes 491528 | tf_op jit(solution)/shard_map/ppermute | solution.py:192
  95.3 14.0 %copy-start = (bf16[8,2,320,256]{3,2,1,0:T(8,128)(2,1)S(1)}, bf16[8,2,320,256]{3,2,1,0:T(8,128)(2,1)}, u32[]{:S(2)}) copy-start(bf16[8,2,320,256]{3,2,1,0:T(8,128)(2,1)} %all_to_all.20.feat_ref.cot_ref) | copy-start | bytes 7864324
  102.5 6.7 %collective-permute-start.2 = (bf16[2,256,432]{2,1,0:T(8,128)(2,1)}, bf16[2,256,432]{2,1,0:T(8,128)(2,1)S(1)}, u32[]{:S(2)}, u32[]{:S(2)}) collective-permute-start(bf16[2,256,432]{2,1,0:T(8,128)(2,1)} %shard_map.121.mine_ref), channel_id=1, source_target_pairs={{0,16},{16,0},{1,17},{17,1},{2,18},{18,2},{3,19},{19,3},{4,20},{20... | collective-permute-start | bytes 1327112 | tf_op jit(solution)/shard_map/ppermute | solution.py:183
  109.3 1.0 copy-start.1
  177.3 29.3 %copy-start.2 = (f32[80,432]{1,0:T(8,128)S(1)}, f32[80,432]{1,0:T(8,128)}, u32[]{:S(2)}) copy-start(f32[80,432]{1,0:T(8,128)} %param.18) | copy-start | bytes 414724
  177.3 29.3 %copy-start.3 = (f32[80,432]{1,0:T(8,128)S(1)}, f32[80,432]{1,0:T(8,128)}, u32[]{:S(2)}) copy-start(f32[80,432]{1,0:T(8,128)} %param.17) | copy-start | bytes 414724
  177.3 29.3 %copy-start.4 = (bf16[80,432]{1,0:T(8,128)(2,1)S(1)}, bf16[80,432]{1,0:T(8,128)(2,1)}, u32[]{:S(2)}) copy-start(bf16[80,432]{1,0:T(8,128)(2,1)} %param.16) | copy-start | bytes 207364
  191.5 14.9 %all-to-all-start.3 = ((f32[32,1,128]{2,1,0:T(1,128)}), f32[32,1,128]{2,1,0:T(1,128)S(1)}, u32[]{:S(2)}, u32[]{:S(2)}) async-start(f32[32,1,128]{2,1,0:T(1,128)} %broadcast_in_dim.11), calls=%async_computation.3 | async-start | bytes 32768 | tf_op jit(solution)/shard_map/all_to_all | solution.py:188
Sparse Core Ops, SparseCore 0:
  10.1 83.1 all-gather.2

commit v2 on v1

--- a/solution.py
+++ b/solution.py
@@ -23,19 +23,24 @@
 MP = ("xh", "z")
 
 COLUMNS = 256
-FORWARD_VMEM = 54 * 1024 * 1024
+FORWARD_VMEM = 52 * 1024 * 1024
 BACKWARD_VMEM = 16 * 1024 * 1024
 
 
-def forward_kernel(feat_ref, w_ref, out_ref, tok_ref):
+def forward_kernel(line_ref, feat_ref, w_ref, out_ref, tok_ref):
     lines, planes, depth, rows = feat_ref.shape
     half = lines // 2
+    line = line_ref[0]
 
     @pl.when(pl.program_id(0) == 0)
     def _():
         for part in range(2 * planes):
             first = half * (part % 2)
-            piece = feat_ref[first : first + half, part // 2].reshape(half * depth, rows)
+            pieces = [
+                feat_ref[lax.rem(first + step + lines - line, lines), part // 2]
+                for step in range(half)
+            ]
+            piece = jnp.concatenate(pieces, axis=0)
             tok_ref[:, part * half * depth : (part + 1) * half * depth] = piece.T
 
     def project(which):
@@ -50,7 +55,7 @@
     out_ref[1] = (silu_slope * up_pre * gate_dot + silu_val * up_dot).astype(jnp.bfloat16)
 
 
-def forward(features, weights):
+def forward(line, features, weights):
     lines, planes, double, rows = features.shape
     shards, _, depth, units = weights.shape
     width = double // 2
@@ -58,20 +63,23 @@
     return pl.pallas_call(
         forward_kernel,
         out_shape=jax.ShapeDtypeStruct((2, rows, units), jnp.bfloat16),
-        grid=(pl.cdiv(units, COLUMNS),),
-        in_specs=[
-            pl.BlockSpec((lines, planes, width, rows), lambda j: (0, 0, 0, 0)),
-            pl.BlockSpec((shards, 4, depth, COLUMNS), lambda j: (0, 0, 0, j)),
-        ],
-        out_specs=pl.BlockSpec((2, rows, COLUMNS), lambda j: (0, 0, j)),
-        scratch_shapes=[pltpu.VMEM((rows, inputs), jnp.bfloat16)],
+        grid_spec=pltpu.PrefetchScalarGridSpec(
+            num_scalar_prefetch=1,
+            grid=(pl.cdiv(units, COLUMNS),),
+            in_specs=[
+                pl.BlockSpec((lines, planes, width, rows), lambda j, line: (0, 0, 0, 0)),
+                pl.BlockSpec((shards, 4, depth, COLUMNS), lambda j, line: (0, 0, 0, j)),
+            ],
+            out_specs=pl.BlockSpec((2, rows, COLUMNS), lambda j, line: (0, 0, j)),
+            scratch_shapes=[pltpu.VMEM((rows, inputs), jnp.bfloat16)],
+        ),
         compiler_params=pltpu.CompilerParams(vmem_limit_bytes=FORWARD_VMEM),
         cost_estimate=pl.CostEstimate(
             flops=2 * rows * inputs * 4 * units,
             bytes_accessed=weights.size * 2 + inputs * rows * 2,
             transcendentals=rows * units,
         ),
-    )(features, weights)
+    )(line, features, weights)
 
 
 def top_column(block):
@@ -87,13 +95,16 @@
     return high, jnp.sum(rest, axis=1, keepdims=True)
 
 
-def backward_kernel(cot_ref, mine_ref, other_ref, out_ref):
-    blocks, _, double, rows = cot_ref.shape
+def backward_kernel(line_ref, cot_ref, mine_ref, other_ref, out_ref):
+    lines, _, double, _ = cot_ref.shape
     depth = double // 2
+    blocks = out_ref.shape[0]
+    first = lax.rem(pl.program_id(0), lines // blocks) * blocks + lines - line_ref[0]
+    pieces = [cot_ref[lax.rem(first + step, lines), 0] for step in range(blocks)]
     sides = []
     for which in range(2):
-        piece = cot_ref[:, 0, which * depth : (which + 1) * depth]
-        sides.append(piece.reshape(blocks * depth, rows))
+        parts = [piece[which * depth : (which + 1) * depth] for piece in pieces]
+        sides.append(jnp.concatenate(parts, axis=0))
 
     def summed(kind):
         total = 0.0
@@ -110,7 +121,7 @@
         out_ref[index] = jnp.concatenate(parts, axis=1).astype(jnp.bfloat16)
 
 
-def backward(features, mine, other):
+def backward(line, features, mine, other):
     lines, planes, double, rows = features.shape
     units = mine.shape[2]
     depth = double // 4
@@ -121,22 +132,25 @@
     return pl.pallas_call(
         backward_kernel,
         out_shape=jax.ShapeDtypeStruct((shards, depth, 2 * units + 2), jnp.bfloat16),
-        grid=(parts,),
-        in_specs=[
-            pl.BlockSpec(
-                (block, 1, double // 2, rows), lambda i: (i % per_plane, i // per_plane, 1, 0)
-            ),
-            pl.BlockSpec(mine.shape, lambda i: (0, 0, 0)),
-            pl.BlockSpec(mine.shape, lambda i: (0, 0, 0)),
-        ],
-        out_specs=pl.BlockSpec((block, depth, 2 * units + 2), lambda i: (i, 0, 0)),
+        grid_spec=pltpu.PrefetchScalarGridSpec(
+            num_scalar_prefetch=1,
+            grid=(parts,),
+            in_specs=[
+                pl.BlockSpec(
+                    (lines, 1, double // 2, rows), lambda i, line: (0, i // per_plane, 1, 0)
+                ),
+                pl.BlockSpec(mine.shape, lambda i, line: (0, 0, 0)),
+                pl.BlockSpec(mine.shape, lambda i, line: (0, 0, 0)),
+            ],
+            out_specs=pl.BlockSpec((block, depth, 2 * units + 2), lambda i, line: (i, 0, 0)),
+        ),
         compiler_params=pltpu.CompilerParams(vmem_limit_bytes=BACKWARD_VMEM),
         cost_estimate=pl.CostEstimate(
             flops=2 * shards * depth * 4 * rows * units,
             bytes_accessed=2 * (features.size // 2 + 2 * mine.size + shards * depth * 2 * units),
             transcendentals=0,
         ),
-    )(features, mine, other)
+    )(line, features, mine, other)
 
 
 def gradient_kernel(packed_ref, gradient_ref, square_ref):
@@ -188,11 +202,23 @@
     return lax.all_to_all(copies, axes, 0, 0, tiled=True)
 
 
-def gather_features(value):
+def pair_features(value):
     other = lax.ppermute(value, "xh", [(0, 1), (1, 0)])
     low = lax.axis_index("xh") == 0
-    pair = jnp.stack([jnp.where(low, value, other), jnp.where(low, other, value)])
-    return to_all(pair, "z")
+    return jnp.stack([jnp.where(low, value, other), jnp.where(low, other, value)])
+
+
+def ring_gather(value):
+    lines = lax.axis_size("z")
+    up = [(place, (place + 1) % lines) for place in range(lines)]
+    down = [(to, start) for start, to in up]
+    below, above = [value], [value]
+    for _ in range(lines // 2 - 1):
+        below.append(lax.ppermute(below[-1], "z", up))
+        above.append(lax.ppermute(above[-1], "z", down))
+    first = lax.ppermute(below[-1][0], "z", up)
+    second = lax.ppermute(above[-1][1], "z", down)
+    return jnp.stack(above + [jnp.stack([first, second])] + below[:0:-1])
 
 
 def sum_over_all(square):
@@ -222,11 +248,13 @@
     cot_t = cotangent.T
     cot_mine = lax.dynamic_slice_in_dim(cot_t, core * shard_rows, shard_rows, 0)
     cot_send = lax.dynamic_slice_in_dim(cot_t, (1 - core) * shard_rows, shard_rows, 0)
-    features = gather_features(jnp.concatenate([tokens.T, cot_mine, swap_cores(cot_send)]))
+    mine = jnp.concatenate([tokens.T, cot_mine, swap_cores(cot_send)])
+    features = ring_gather(pair_features(mine))
     weights, features = lax.optimization_barrier((weights, features))
 
-    hidden = forward(features, weights)
-    packed = backward(features, hidden, swap_cores(hidden))
+    line = lax.axis_index("z").reshape(1)
+    hidden = forward(line, features, weights)
+    packed = backward(line, features, hidden, swap_cores(hidden))
     packed = lax.all_to_all(packed, CHIPS, 0, 0, tiled=True)
     gradient, square = gradient_sum(packed, units)
     norm_total = sum_over_all(square)

time: 215 us -> 213 us (level)
  blocking collectives: 140 us -> 78.1 us
  waiting for transfers between devices: 13.1 us -> 46.8 us
  starting transfers between devices: 22.7 us -> 46.6 us
  local copies, waits for them, and re-layouts: 2.74 us -> 5.32 us
    all_to_all x2 -> x1, blocking collectives: 77.3 us -> 18.2 us  [to_all(): return lax.all_to_all(copies, axes, 0, 0, tiled=True)]
    ppermute x1 -> x9, starting transfers between devices: 1.92 us -> 28.8 us  [the longest x3 14.4 us: ring_gather(): above.append(lax.ppermute(above[-1], 'z', down))]
    all_gather x1, waiting for transfers between devices: 0.01 us -> 20.4 us  [per_device(): lax.all_gather(jnp.stack([gate_weight, up_weight, probe_gate, probe_up]),...]
    ppermute x1 -> x9, waiting for transfers between devices: 6.9 us -> 20.3 us  [the longest x3 11.2 us: ring_gather(): below.append(lax.ppermute(below[-1], 'z', up))]
    ppermute x2, starting transfers between devices: 13.8 us -> 11 us  [swap_cores(): return lax.ppermute(value, 'core', [(0, 1), (1, 0)])]
    unnamed x10 -> x15, local copies, waits for them, and re-layouts: 1.06 us -> 3.84 us
    all_to_all x1, blocking collectives: 62.4 us -> 59.9 us  [per_device(): packed = lax.all_to_all(packed, CHIPS, 0, 0, tiled=True)]
  transfers between devices with their start and end apart: 5 -> 13, of which waited for: 4 -> 10; matrix products, arithmetic and copies ran while one was open for 1% -> 2% of each run, Pallas kernels for 2% -> 2%
where the time goes in v2:
time: 213 us; the launch traced here: 212 us
  blocking collectives  78.1 us (37%)
  waiting for transfers between devices  46.8 us (22%)
  starting transfers between devices  46.6 us (22%)
  Pallas kernels  15.7 us (7%)
  between operations  15.2 us (7%)
  local copies, waits for them, and re-layouts  5.32 us (2%)
  other arithmetic  4.56 us (2%)
    all_to_all x1, blocking collectives, per_device(): packed = lax.all_to_all(packed, CHIPS, 0, 0, tiled=True)  59.9 us
    all_gather x1, waiting for transfers between devices, per_device(): lax.all_gather(jnp.stack([gate_weight, up_weight, probe_gate, probe_up]),...  20.4 us
    all_to_all x1, blocking collectives, to_all(): return lax.all_to_all(copies, axes, 0, 0, tiled=True)  18.2 us
    ppermute x3, starting transfers between devices, ring_gather(): above.append(lax.ppermute(above[-1], 'z', down))  14.4 us
    ppermute x3, waiting for transfers between devices, ring_gather(): below.append(lax.ppermute(below[-1], 'z', up))  11.2 us
    ppermute x2, starting transfers between devices, swap_cores(): return lax.ppermute(value, 'core', [(0, 1), (1, 0)])  11 us
    ppermute x1, waiting for transfers between devices, pair_features(): other = lax.ppermute(value, 'xh', [(0, 1), (1, 0)])  6.9 us
    all_to_all x1, starting transfers between devices, to_all(): return lax.all_to_all(copies, axes, 0, 0, tiled=True)  6.84 us
  transfers between devices with their start and end apart: 13, of which 10 were waited for; matrix products, arithmetic and copies ran while one was open for 2% of the time, Pallas kernels for 2%

profile of v2, /device:TPU:1, one launch (start us, length us, event | category | flops | bytes accessed | tf_op | source)
XLA Modules:
  0.0 212.2 jit_solution(10700709938876025046)
XLA Ops:
  7.2 1.8 pad_maximum_fusion
  9.9 8.8 %collective-permute-start = (bf16[80,256]{1,0:T(8,128)(2,1)S(1)}, bf16[80,256]{1,0:T(8,128)(2,1)S(1)}, u32[]{:S(2)}, u32[]{:S(2)}) collective-permute-start(bf16[80,256]{1,0:T(8,128)(2,1)S(1)} %get-tuple-element.17), channel_id=1, source_target_pairs={{0,16},{16,0},{1,17},{17,1},{2,18},{18,2},{3,19},{19,3},{4,20},{20... | collective-permute-start | bytes 122888 | tf_op jit(solution)/shard_map/ppermute | solution.py:197
  19.5 0.9 pad_maximum_fusion.2
  20.4 1.9 collective-permute-start.1
  22.3 6.9 %collective-permute-done.1 = bf16[320,256]{1,0:T(8,128)(2,1)S(1)} collective-permute-done((bf16[320,256]{1,0:T(8,128)(2,1)S(1)}, bf16[320,256]{1,0:T(8,128)(2,1)S(1)}, u32[]{:S(2)}, u32[]{:S(2)}) %collective-permute-start.1) | collective-permute-done | bytes 163872 | tf_op jit(solution)/shard_map/ppermute | solution.py:206
  29.2 0.9 select_bitcast_fusion.1
  30.2 1.9 collective-permute-start.5
  32.1 5.3 %collective-permute-start.2 = (bf16[2,320,256]{2,1,0:T(8,128)(2,1)S(1)}, bf16[2,320,256]{2,1,0:T(8,128)(2,1)}, u32[]{:S(2)}, u32[]{:S(2)}) collective-permute-start(bf16[2,320,256]{2,1,0:T(8,128)(2,1)S(1)} %pad_maximum_fusion.1), channel_id=1, source_target_pairs={{1,0},{2,1},{3,2},{4,3},{5,4},{6,5},{7,6},{0,7},{9,8},{10,9},{11,1... | collective-permute-start | bytes 983048 | tf_op jit(solution)/shard_map/ppermute | solution.py:218
  37.5 4.9 %collective-permute-done.5 = bf16[2,320,256]{2,1,0:T(8,128)(2,1)S(1)} collective-permute-done((bf16[2,320,256]{2,1,0:T(8,128)(2,1)S(1)}, bf16[2,320,256]{2,1,0:T(8,128)(2,1)S(1)}, u32[]{:S(2)}, u32[]{:S(2)}) %collective-permute-start.5) | collective-permute-done | bytes 327712 | tf_op jit(solution)/shard_map/ppermute | solution.py:217
  42.4 1.9 collective-permute-start.6
  44.3 4.6 %collective-permute-start.3 = (bf16[2,320,256]{2,1,0:T(8,128)(2,1)}, bf16[2,320,256]{2,1,0:T(8,128)(2,1)S(1)}, u32[]{:S(2)}, u32[]{:S(2)}) collective-permute-start(bf16[2,320,256]{2,1,0:T(8,128)(2,1)} %collective-permute-done.2), channel_id=1, source_target_pairs={{1,0},{2,1},{3,2},{4,3},{5,4},{6,5},{7,6},{0,7},{9,8},{10,9},{11,1... | collective-permute-start | bytes 983048 | tf_op jit(solution)/shard_map/ppermute | solution.py:218
  48.9 4.1 %collective-permute-done.6 = bf16[2,320,256]{2,1,0:T(8,128)(2,1)} collective-permute-done((bf16[2,320,256]{2,1,0:T(8,128)(2,1)S(1)}, bf16[2,320,256]{2,1,0:T(8,128)(2,1)}, u32[]{:S(2)}, u32[]{:S(2)}) %collective-permute-start.6) | collective-permute-done | bytes 327712 | tf_op jit(solution)/shard_map/ppermute | solution.py:217
  53.0 1.9 collective-permute-start.7
  54.9 1.0 bitcast_dynamic-update-slice_fusion.5
  55.9 4.6 %collective-permute-start.4 = (bf16[2,320,256]{2,1,0:T(8,128)(2,1)S(1)}, bf16[2,320,256]{2,1,0:T(8,128)(2,1)S(1)}, u32[]{:S(2)}, u32[]{:S(2)}) collective-permute-start(bf16[2,320,256]{2,1,0:T(8,128)(2,1)S(1)} %collective-permute-done.3), channel_id=1, source_target_pairs={{1,0},{2,1},{3,2},{4,3},{5,4},{6,5},{7,6},{0,7},{9,8},{10,9},{11,1... | collective-permute-start | bytes 983048 | tf_op jit(solution)/shard_map/ppermute | solution.py:218
  60.5 2.2 %collective-permute-done.7 = bf16[2,320,256]{2,1,0:T(8,128)(2,1)S(1)} collective-permute-done((bf16[2,320,256]{2,1,0:T(8,128)(2,1)}, bf16[2,320,256]{2,1,0:T(8,128)(2,1)S(1)}, u32[]{:S(2)}, u32[]{:S(2)}) %collective-permute-start.7) | collective-permute-done | bytes 327712 | tf_op jit(solution)/shard_map/ppermute | solution.py:217
  62.8 1.9 collective-permute-start.8
  64.7 4.8 %collective-permute-start.9 = (bf16[320,256]{1,0:T(8,128)(2,1)S(1)}, bf16[320,256]{1,0:T(8,128)(2,1)S(1)}, u32[]{:S(2)}, u32[]{:S(2)}) collective-permute-start(bf16[320,256]{1,0:T(8,128)(2,1)S(1)} %slice_bitcast_fusion), channel_id=1, source_target_pairs={{1,0},{2,1},{3,2},{4,3},{5,4},{6,5},{7,6},{0,7},{9,8},{10,9},{11,1... | collective-permute-start | bytes 491528 | tf_op jit(solution)/shard_map/ppermute | solution.py:220
  70.0 1.7 collective-permute-done.9
  71.8 1.0 bitcast_dynamic-update-slice_fusion.1
  72.9 20.4 %all-gather.3.cloned.1.call-done = bf16[128,80,432]{2,1,0:T(8,128)(2,1)} async-done(((bf16[4,80,432]{2,1,0:T(8,128)(2,1)}), bf16[128,80,432]{2,1,0:T(8,128)(2,1)}) %all-gather.3.cloned.1.call-update) | async-done | bytes 8847376 | tf_op jit(solution)/shard_map/all_gather | solution.py:245
  93.2 6.4 %shard_map.121.mine_ref = bf16[2,256,432]{2,1,0:T(8,128)(2,1)S(1)} custom-call(s32[1]{0:T(128)} %bitcast.line_ref, bf16[8,2,320,256]{3,2,1,0:T(8,128)(2,1)} %copy-done, bf16[32,4,80,432]{3,2,1,0:T(8,128)(2,1)} %bitcast.46), custom_call_target="tpu_custom_call" | custom-call | flops 2264924160 | bytes 10158080 | tf_op jit(solution)/shard_map/pallas_call | solution.py:63
  99.6 2.2 %collective-permute-start.10 = (bf16[2,256,432]{2,1,0:T(8,128)(2,1)S(1)}, bf16[2,256,432]{2,1,0:T(8,128)(2,1)S(1)}, u32[]{:S(2)}, u32[]{:S(2)}) collective-permute-start(bf16[2,256,432]{2,1,0:T(8,128)(2,1)S(1)} %shard_map.121.mine_ref), channel_id=1, source_target_pairs={{0,16},{16,0},{1,17},{17,1},{2,18},{18,2},{3,19},{19,3},{4,20},{20... | collective-permute-start | bytes 1327112 | tf_op jit(solution)/shard_map/ppermute | solution.py:197
  101.8 1.6 collective-permute-done.10.other_ref
  103.4 1.7 copy-done.1
  105.2 4.6 %shard_map.122 = bf16[16,80,866]{2,1,0:T(8,128)(2,1)S(1)} custom-call(s32[1]{0:T(128)} %bitcast.line_ref, bf16[8,2,320,256]{3,2,1,0:T(8,128)(2,1)S(1)} %copy-done.1, bf16[2,256,432]{2,1,0:T(8,128)(2,1)S(1)} %shard_map.121.mine_ref, bf16[2,256,432]{2,1,0:T(8,128)(2,1)S(1)} %collective-permute-done.10.other_ref), custom_call_target="tpu_custom_call" | custom-call | flops 1132462080 | bytes 4407296 | tf_op jit(solution)/shard_map/pallas_call | solution.py:132
  109.8 59.9 %all_to_all.15.packed_ref = bf16[16,80,866]{2,1,0:T(8,128)(2,1)S(1)} all-to-all(bf16[16,80,866]{2,1,0:T(8,128)(2,1)S(1)} %shard_map.122), channel_id=1, replica_groups=mesh['y'=8,'xl'=2,'core'=2,'xh'=2,'z'=8] {'y','xl'}, dimensions={0} | all-to-all | bytes 4433920 | tf_op jit(solution)/shard_map/all_to_all | solution.py:258
  169.6 1.1 shard_map.123
  170.8 18.2 %all_to_all.16 = f32[16,1,128]{2,1,0:T(1,128)S(1)} all-to-all(f32[16,1,128]{2,1,0:T(1,128)S(1)} %broadcast_in_dim.7), channel_id=1, replica_groups=mesh['y'=8,'xl'=2,'core'=2,'xh'=2,'z'=8] {'xh','z'}, dimensions={0} | all-to-all | bytes 16384 | tf_op jit(solution)/shard_map/all_to_all | solution.py:202
  189.6 6.8 %all-to-all-start.2 = ((f32[32,1,128]{2,1,0:T(1,128)}), f32[32,1,128]{2,1,0:T(1,128)S(1)}, u32[]{:S(2)}, u32[]{:S(2)}) async-start(f32[32,1,128]{2,1,0:T(1,128)} %broadcast_in_dim.16), calls=%async_computation.2 | async-start | bytes 32768 | tf_op jit(solution)/shard_map/all_to_all | solution.py:202
  197.2 3.6 %shard_map.124 = f32[80,432]{1,0:T(8,128)S(1)} custom-call(bf16[16,80,866]{2,1,0:T(8,128)(2,1)S(1)} %all_to_all.15.packed_ref), custom_call_target="tpu_custom_call" | custom-call | tf_op jit(solution)/shard_map/pallas_call | solution.py:189
  200.8 3.6 %all-to-all-done.2 = f32[32,1,128]{2,1,0:T(1,128)S(1)} async-done(((f32[32,1,128]{2,1,0:T(1,128)}), f32[32,1,128]{2,1,0:T(1,128)S(1)}, u32[]{:S(2)}, u32[]{:S(2)}) %all-to-all-start.2) | async-done | bytes 16416 | tf_op jit(solution)/shard_map/all_to_all | solution.py:202
  (31 shorter events, 3.9 us)
Async XLA Ops:
  7.2 86.1 %all-gather.3.cloned.1.call-start = ((), (), s32[]{:S(2)}) async-start(), calls=%async_computation.3 | async-start | bytes 10813440 | tf_op jit(solution)/shard_map/all_gather | solution.py:245
  9.9 9.6 %collective-permute-start = (bf16[80,256]{1,0:T(8,128)(2,1)S(1)}, bf16[80,256]{1,0:T(8,128)(2,1)S(1)}, u32[]{:S(2)}, u32[]{:S(2)}) collective-permute-start(bf16[80,256]{1,0:T(8,128)(2,1)S(1)} %get-tuple-element.17), channel_id=1, source_target_pairs={{0,16},{16,0},{1,17},{17,1},{2,18},{18,2},{3,19},{19,3},{4,20},{20... | collective-permute-start | bytes 122888 | tf_op jit(solution)/shard_map/ppermute | solution.py:197
  20.4 8.8 %collective-permute-start.1 = (bf16[320,256]{1,0:T(8,128)(2,1)S(1)}, bf16[320,256]{1,0:T(8,128)(2,1)S(1)}, u32[]{:S(2)}, u32[]{:S(2)}) collective-permute-start(bf16[320,256]{1,0:T(8,128)(2,1)S(1)} %pad_maximum_fusion.2), channel_id=1, source_target_pairs={{0,8},{8,0},{1,9},{9,1},{2,10},{10,2},{3,11},{11,3},{4,12},{12,4},... | collective-permute-start | bytes 491528 | tf_op jit(solution)/shard_map/ppermute | solution.py:206
  30.2 12.1 %collective-permute-start.5 = (bf16[2,320,256]{2,1,0:T(8,128)(2,1)S(1)}, bf16[2,320,256]{2,1,0:T(8,128)(2,1)S(1)}, u32[]{:S(2)}, u32[]{:S(2)}) collective-permute-start(bf16[2,320,256]{2,1,0:T(8,128)(2,1)S(1)} %pad_maximum_fusion.1), channel_id=1, source_target_pairs={{0,1},{1,2},{2,3},{3,4},{4,5},{5,6},{6,7},{7,0},{8,9},{9,10},{10,1... | collective-permute-start | bytes 983048 | tf_op jit(solution)/shard_map/ppermute | solution.py:217
  32.1 12.1 %collective-permute-start.2 = (bf16[2,320,256]{2,1,0:T(8,128)(2,1)S(1)}, bf16[2,320,256]{2,1,0:T(8,128)(2,1)}, u32[]{:S(2)}, u32[]{:S(2)}) collective-permute-start(bf16[2,320,256]{2,1,0:T(8,128)(2,1)S(1)} %pad_maximum_fusion.1), channel_id=1, source_target_pairs={{1,0},{2,1},{3,2},{4,3},{5,4},{6,5},{7,6},{0,7},{9,8},{10,9},{11,1... | collective-permute-start | bytes 983048 | tf_op jit(solution)/shard_map/ppermute | solution.py:218
  42.4 10.6 %collective-permute-start.6 = (bf16[2,320,256]{2,1,0:T(8,128)(2,1)S(1)}, bf16[2,320,256]{2,1,0:T(8,128)(2,1)}, u32[]{:S(2)}, u32[]{:S(2)}) collective-permute-start(bf16[2,320,256]{2,1,0:T(8,128)(2,1)S(1)} %collective-permute-done.5), channel_id=1, source_target_pairs={{0,1},{1,2},{2,3},{3,4},{4,5},{5,6},{6,7},{7,0},{8,9},{9,10},{10,1... | collective-permute-start | bytes 983048 | tf_op jit(solution)/shard_map/ppermute | solution.py:217
  44.3 11.6 %collective-permute-start.3 = (bf16[2,320,256]{2,1,0:T(8,128)(2,1)}, bf16[2,320,256]{2,1,0:T(8,128)(2,1)S(1)}, u32[]{:S(2)}, u32[]{:S(2)}) collective-permute-start(bf16[2,320,256]{2,1,0:T(8,128)(2,1)} %collective-permute-done.2), channel_id=1, source_target_pairs={{1,0},{2,1},{3,2},{4,3},{5,4},{6,5},{7,6},{0,7},{9,8},{10,9},{11,1... | collective-permute-start | bytes 983048 | tf_op jit(solution)/shard_map/ppermute | solution.py:218
  53.0 9.8 %collective-permute-start.7 = (bf16[2,320,256]{2,1,0:T(8,128)(2,1)}, bf16[2,320,256]{2,1,0:T(8,128)(2,1)S(1)}, u32[]{:S(2)}, u32[]{:S(2)}) collective-permute-start(bf16[2,320,256]{2,1,0:T(8,128)(2,1)} %collective-permute-done.6), channel_id=1, source_target_pairs={{0,1},{1,2},{2,3},{3,4},{4,5},{5,6},{6,7},{7,0},{8,9},{9,10},{10,1... | collective-permute-start | bytes 983048 | tf_op jit(solution)/shard_map/ppermute | solution.py:217
  55.9 8.8 %collective-permute-start.4 = (bf16[2,320,256]{2,1,0:T(8,128)(2,1)S(1)}, bf16[2,320,256]{2,1,0:T(8,128)(2,1)S(1)}, u32[]{:S(2)}, u32[]{:S(2)}) collective-permute-start(bf16[2,320,256]{2,1,0:T(8,128)(2,1)S(1)} %collective-permute-done.3), channel_id=1, source_target_pairs={{1,0},{2,1},{3,2},{4,3},{5,4},{6,5},{7,6},{0,7},{9,8},{10,9},{11,1... | collective-permute-start | bytes 983048 | tf_op jit(solution)/shard_map/ppermute | solution.py:218
  62.8 7.3 %collective-permute-start.8 = (bf16[320,256]{1,0:T(8,128)(2,1)S(1)}, bf16[320,256]{1,0:T(8,128)(2,1)S(1)}, u32[]{:S(2)}, u32[]{:S(2)}) collective-permute-start(bf16[320,256]{1,0:T(8,128)(2,1)S(1)} %slice_bitcast_fusion.1), channel_id=1, source_target_pairs={{0,1},{1,2},{2,3},{3,4},{4,5},{5,6},{6,7},{7,0},{8,9},{9,10},{10,1... | collective-permute-start | bytes 491528 | tf_op jit(solution)/shard_map/ppermute | solution.py:219
  64.7 7.0 %collective-permute-start.9 = (bf16[320,256]{1,0:T(8,128)(2,1)S(1)}, bf16[320,256]{1,0:T(8,128)(2,1)S(1)}, u32[]{:S(2)}, u32[]{:S(2)}) collective-permute-start(bf16[320,256]{1,0:T(8,128)(2,1)S(1)} %slice_bitcast_fusion), channel_id=1, source_target_pairs={{1,0},{2,1},{3,2},{4,3},{5,4},{6,5},{7,6},{0,7},{9,8},{10,9},{11,1... | collective-permute-start | bytes 491528 | tf_op jit(solution)/shard_map/ppermute | solution.py:220
  72.9 20.4 %copy-start = (bf16[8,2,320,256]{3,2,1,0:T(8,128)(2,1)}, bf16[8,2,320,256]{3,2,1,0:T(8,128)(2,1)S(1)}, u32[]{:S(2)}) copy-start(bf16[8,2,320,256]{3,2,1,0:T(8,128)(2,1)S(1)} %bitcast_dynamic-update-slice_fusion.feat_ref.cot_ref) | copy-start | bytes 7864324
  99.6 3.8 %collective-permute-start.10 = (bf16[2,256,432]{2,1,0:T(8,128)(2,1)S(1)}, bf16[2,256,432]{2,1,0:T(8,128)(2,1)S(1)}, u32[]{:S(2)}, u32[]{:S(2)}) collective-permute-start(bf16[2,256,432]{2,1,0:T(8,128)(2,1)S(1)} %shard_map.121.mine_ref), channel_id=1, source_target_pairs={{0,16},{16,0},{1,17},{17,1},{2,18},{18,2},{3,19},{19,3},{4,20},{20... | collective-permute-start | bytes 1327112 | tf_op jit(solution)/shard_map/ppermute | solution.py:197
  103.4 1.7 copy-start.1
  169.6 34.9 %copy-start.2 = (f32[80,432]{1,0:T(8,128)S(1)}, f32[80,432]{1,0:T(8,128)}, u32[]{:S(2)}) copy-start(f32[80,432]{1,0:T(8,128)} %param.18) | copy-start | bytes 414724
  169.6 34.9 %copy-start.3 = (f32[80,432]{1,0:T(8,128)S(1)}, f32[80,432]{1,0:T(8,128)}, u32[]{:S(2)}) copy-start(f32[80,432]{1,0:T(8,128)} %param.17) | copy-start | bytes 414724
  169.6 34.9 %copy-start.4 = (bf16[80,432]{1,0:T(8,128)(2,1)S(1)}, bf16[80,432]{1,0:T(8,128)(2,1)}, u32[]{:S(2)}) copy-start(bf16[80,432]{1,0:T(8,128)(2,1)} %param.16) | copy-start | bytes 207364
  189.6 14.8 %all-to-all-start.2 = ((f32[32,1,128]{2,1,0:T(1,128)}), f32[32,1,128]{2,1,0:T(1,128)S(1)}, u32[]{:S(2)}, u32[]{:S(2)}) async-start(f32[32,1,128]{2,1,0:T(1,128)} %broadcast_in_dim.16), calls=%async_computation.2 | async-start | bytes 32768 | tf_op jit(solution)/shard_map/all_to_all | solution.py:202
Sparse Core Ops, SparseCore 0:
  10.1 83.0 all-gather.2

commit v3 on v2

--- a/solution.py
+++ b/solution.py
@@ -23,13 +23,15 @@
 MP = ("xh", "z")
 
 COLUMNS = 256
+PADDED = 48
 FORWARD_VMEM = 52 * 1024 * 1024
-BACKWARD_VMEM = 16 * 1024 * 1024
+BACKWARD_VMEM = 24 * 1024 * 1024
 
 
 def forward_kernel(line_ref, feat_ref, w_ref, out_ref, tok_ref):
-    lines, planes, depth, rows = feat_ref.shape
+    lines, planes, _, rows = feat_ref.shape
     half = lines // 2
+    depth = tok_ref.shape[1] // (lines * planes)
     line = line_ref[0]
 
     @pl.when(pl.program_id(0) == 0)
@@ -37,7 +39,7 @@
         for part in range(2 * planes):
             first = half * (part % 2)
             pieces = [
-                feat_ref[lax.rem(first + step + lines - line, lines), part // 2]
+                feat_ref[lax.rem(first + step + lines - line, lines), part // 2, :depth]
                 for step in range(half)
             ]
             piece = jnp.concatenate(pieces, axis=0)
@@ -56,10 +58,9 @@
 
 
 def forward(line, features, weights):
-    lines, planes, double, rows = features.shape
+    lines, planes, _, rows = features.shape
     shards, _, depth, units = weights.shape
-    width = double // 2
-    inputs = lines * planes * width
+    inputs = shards * depth
     return pl.pallas_call(
         forward_kernel,
         out_shape=jax.ShapeDtypeStruct((2, rows, units), jnp.bfloat16),
@@ -67,7 +68,7 @@
             num_scalar_prefetch=1,
             grid=(pl.cdiv(units, COLUMNS),),
             in_specs=[
-                pl.BlockSpec((lines, planes, width, rows), lambda j, line: (0, 0, 0, 0)),
+                pl.BlockSpec(features.shape, lambda j, line: (0, 0, 0, 0)),
                 pl.BlockSpec((shards, 4, depth, COLUMNS), lambda j, line: (0, 0, 0, j)),
             ],
             out_specs=pl.BlockSpec((2, rows, COLUMNS), lambda j, line: (0, 0, j)),
@@ -95,72 +96,73 @@
     return high, jnp.sum(rest, axis=1, keepdims=True)
 
 
-def backward_kernel(line_ref, cot_ref, mine_ref, other_ref, out_ref):
-    lines, _, double, _ = cot_ref.shape
-    depth = double // 2
-    blocks = out_ref.shape[0]
-    first = lax.rem(pl.program_id(0), lines // blocks) * blocks + lines - line_ref[0]
-    pieces = [cot_ref[lax.rem(first + step, lines), 0] for step in range(blocks)]
-    sides = []
-    for which in range(2):
-        parts = [piece[which * depth : (which + 1) * depth] for piece in pieces]
-        sides.append(jnp.concatenate(parts, axis=0))
+def backward_kernel(line_ref, feat_ref, *refs):
+    out_ref, groups = refs[-1], refs[:-1]
+    lines, _, width, _ = feat_ref.shape
+    start = width - len(groups) * PADDED
+    first = lines - line_ref[0]
+    pieces = [feat_ref[lax.rem(first + step, lines), 0] for step in range(lines)]
 
     def summed(kind):
         total = 0.0
-        for cot, ref in zip(sides, (mine_ref, other_ref)):
+        for index, ref in enumerate(groups):
+            begin = start + index * PADDED
+            cot = jnp.concatenate([piece[begin : begin + PADDED] for piece in pieces], axis=0)
             partial = jnp.dot(cot, ref[kind], preferred_element_type=jnp.float32) * (1.0 / TOKENS)
             total += partial.astype(jnp.bfloat16).astype(jnp.float32)
         return total
 
     totals = [summed(kind) for kind in range(2)]
-    for index in range(blocks):
+    for index in range(lines):
+        begin = index * PADDED
         parts = []
         for total in totals:
-            parts += rounded_with_rest(total[index * depth : (index + 1) * depth])
+            parts += rounded_with_rest(total[begin : begin + out_ref.shape[1]])
         out_ref[index] = jnp.concatenate(parts, axis=1).astype(jnp.bfloat16)
 
 
-def backward(line, features, mine, other):
-    lines, planes, double, rows = features.shape
-    units = mine.shape[2]
-    depth = double // 4
+def backward(line, features, groups, depth):
+    lines, planes, width, rows = features.shape
+    units = groups[0].shape[2]
     shards = lines * planes
-    parts = 4
-    block = shards // parts
-    per_plane = parts // planes
+    hidden_spec = pl.BlockSpec(groups[0].shape, lambda i, line: (0, 0, 0))
     return pl.pallas_call(
         backward_kernel,
         out_shape=jax.ShapeDtypeStruct((shards, depth, 2 * units + 2), jnp.bfloat16),
         grid_spec=pltpu.PrefetchScalarGridSpec(
             num_scalar_prefetch=1,
-            grid=(parts,),
+            grid=(planes,),
             in_specs=[
-                pl.BlockSpec(
-                    (lines, 1, double // 2, rows), lambda i, line: (0, i // per_plane, 1, 0)
-                ),
-                pl.BlockSpec(mine.shape, lambda i, line: (0, 0, 0)),
-                pl.BlockSpec(mine.shape, lambda i, line: (0, 0, 0)),
+                pl.BlockSpec((lines, 1, width, rows), lambda i, line: (0, i, 0, 0)),
+                *[hidden_spec for _ in groups],
             ],
-            out_specs=pl.BlockSpec((block, depth, 2 * units + 2), lambda i, line: (i, 0, 0)),
+            out_specs=pl.BlockSpec((lines, depth, 2 * units + 2), lambda i, line: (i, 0, 0)),
         ),
         compiler_params=pltpu.CompilerParams(vmem_limit_bytes=BACKWARD_VMEM),
         cost_estimate=pl.CostEstimate(
-            flops=2 * shards * depth * 4 * rows * units,
-            bytes_accessed=2 * (features.size // 2 + 2 * mine.size + shards * depth * 2 * units),
+            flops=2 * shards * PADDED * len(groups) * rows * 2 * units,
+            bytes_accessed=2 * (features.size + 4 * groups[0].size + shards * depth * 2 * units),
             transcendentals=0,
         ),
-    )(line, features, mine, other)
+    )(line, features, *groups)
+
+
+def add_up(packed_ref, out_ref, begin):
+    depth = packed_ref.shape[1]
+    units = out_ref.shape[1]
+    for side in range(2):
+        total = jnp.zeros((depth, units), jnp.float32)
+        for index in range(side, packed_ref.shape[0], 2):
+            block = packed_ref[index].astype(jnp.float32)
+            high = block[:, begin : begin + units]
+            rest = block[:, begin + units : begin + units + 1]
+            total += high + jnp.where(top_column(high), rest, 0.0)
+        out_ref[side * depth : (side + 1) * depth] = total
 
 
 def gradient_kernel(packed_ref, gradient_ref, square_ref):
-    units = gradient_ref.shape[1]
-    total = jnp.zeros(gradient_ref.shape, jnp.float32)
-    for index in range(packed_ref.shape[0]):
-        block = packed_ref[index].astype(jnp.float32)
-        high, rest = block[:, :units], block[:, units : units + 1]
-        total += high + jnp.where(top_column(high), rest, 0.0)
-    gradient_ref[...] = total
+    add_up(packed_ref, gradient_ref, 0)
+    total = gradient_ref[...]
     square_ref[...] = jnp.full(square_ref.shape, jnp.sum(total * total))
 
 
@@ -168,7 +170,7 @@
     return pl.pallas_call(
         gradient_kernel,
         out_shape=(
-            jax.ShapeDtypeStruct((packed.shape[1], units), jnp.float32),
+            jax.ShapeDtypeStruct((2 * packed.shape[1], units), jnp.float32),
             jax.ShapeDtypeStruct((1, 128), jnp.float32),
         ),
         compiler_params=pltpu.CompilerParams(vmem_limit_bytes=BACKWARD_VMEM),
@@ -176,25 +178,26 @@
 
 
 def hessian_kernel(packed_ref, out_ref):
-    units = out_ref.shape[1]
-    total = jnp.zeros(out_ref.shape, jnp.float32)
-    for index in range(packed_ref.shape[0]):
-        block = packed_ref[index].astype(jnp.float32)
-        high, rest = block[:, units + 1 : 2 * units + 1], block[:, 2 * units + 1 :]
-        total += high + jnp.where(top_column(high), rest, 0.0)
-    out_ref[...] = total
+    add_up(packed_ref, out_ref, out_ref.shape[1] + 1)
 
 
 def hessian_sum(packed, units):
     return pl.pallas_call(
         hessian_kernel,
-        out_shape=jax.ShapeDtypeStruct((packed.shape[1], units), jnp.float32),
+        out_shape=jax.ShapeDtypeStruct((2 * packed.shape[1], units), jnp.float32),
         compiler_params=pltpu.CompilerParams(vmem_limit_bytes=BACKWARD_VMEM),
     )(packed)
 
 
-def swap_cores(value):
-    return lax.ppermute(value, "core", [(0, 1), (1, 0)])
+def swap(value, axis):
+    return lax.ppermute(value, axis, [(0, 1), (1, 0)])
+
+
+def share(value, axis):
+    place = lax.axis_index(axis)
+    mine = lax.dynamic_index_in_dim(value, place, 0, keepdims=False)
+    send = lax.dynamic_index_in_dim(value, 1 - place, 0, keepdims=False)
+    return jnp.stack([mine, swap(send, axis)])
 
 
 def to_all(value, axes):
@@ -203,7 +206,7 @@
 
 
 def pair_features(value):
-    other = lax.ppermute(value, "xh", [(0, 1), (1, 0)])
+    other = swap(value, "xh")
     low = lax.axis_index("xh") == 0
     return jnp.stack([jnp.where(low, value, other), jnp.where(low, other, value)])
 
@@ -239,22 +242,24 @@
     curvature,
     step_count,
 ):
-    core = lax.axis_index("core")
     shard_rows, units = gate_weight.shape
 
     weights = lax.all_gather(
         jnp.stack([gate_weight, up_weight, probe_gate, probe_up]), DP, axis=0, tiled=False
     )
-    cot_t = cotangent.T
-    cot_mine = lax.dynamic_slice_in_dim(cot_t, core * shard_rows, shard_rows, 0)
-    cot_send = lax.dynamic_slice_in_dim(cot_t, (1 - core) * shard_rows, shard_rows, 0)
-    mine = jnp.concatenate([tokens.T, cot_mine, swap_cores(cot_send)])
-    features = ring_gather(pair_features(mine))
+    rows = tokens.shape[0]
+    depth = shard_rows // 2
+    cot = cotangent.T.reshape(2, 2, depth, rows).swapaxes(0, 1)
+    cot = share(share(cot, "xl").swapaxes(0, 1), "core")
+    cot = jnp.pad(cot, ((0, 0), (0, 0), (0, PADDED - depth), (0, 0))).reshape(-1, rows)
+    features = ring_gather(pair_features(jnp.concatenate([tokens.T, cot])))
     weights, features = lax.optimization_barrier((weights, features))
 
     line = lax.axis_index("z").reshape(1)
     hidden = forward(line, features, weights)
-    packed = backward(line, features, hidden, swap_cores(hidden))
+    far = swap(hidden, "xl")
+    groups = (hidden, far, swap(hidden, "core"), swap(far, "core"))
+    packed = backward(line, features, groups, depth)
     packed = lax.all_to_all(packed, CHIPS, 0, 0, tiled=True)
     gradient, square = gradient_sum(packed, units)
     norm_total = sum_over_all(square)

time: 213 us -> 204 us (0.958)
  blocking collectives: 78.1 us -> 53.4 us
  starting transfers between devices: 46.6 us -> 58.8 us
  waiting for transfers between devices: 46.8 us -> 50.5 us
    all_to_all x1, blocking collectives: 59.9 us -> 35.3 us  [per_device(): packed = lax.all_to_all(packed, CHIPS, 0, 0, tiled=True)]
    ppermute x3 -> x6, waiting for transfers between devices: 9.36 us -> 22.4 us  [swap(): return lax.ppermute(value, axis, [(0, 1), (1, 0)])]
    all_gather x1, waiting for transfers between devices: 20.4 us -> 8.18 us  [per_device(): lax.all_gather(jnp.stack([gate_weight, up_weight, probe_gate, probe_up]),...]
    ppermute x3 -> x6, starting transfers between devices: 12.9 us -> 23.4 us  [swap(): return lax.ppermute(value, axis, [(0, 1), (1, 0)])]
  transfers between devices with their start and end apart: 13 -> 16, of which waited for: 10 -> 12; matrix products, arithmetic and copies ran while one was open for 2% -> 3% of each run, Pallas kernels for 2% -> 1%
where the time goes in v3:
time: 204 us; the launch traced here: 203 us
  starting transfers between devices  58.8 us (29%)
  blocking collectives  53.4 us (26%)
  waiting for transfers between devices  50.5 us (25%)
  between operations  15.2 us (7%)
  Pallas kernels  14.3 us (7%)
  local copies, waits for them, and re-layouts  6.44 us (3%)
  other arithmetic  4.55 us (2%)
    all_to_all x1, blocking collectives, per_device(): packed = lax.all_to_all(packed, CHIPS, 0, 0, tiled=True)  35.3 us
    ppermute x6, starting transfers between devices, swap(): return lax.ppermute(value, axis, [(0, 1), (1, 0)])  23.4 us
    ppermute x6, waiting for transfers between devices, swap(): return lax.ppermute(value, axis, [(0, 1), (1, 0)])  22.4 us
    all_to_all x1, blocking collectives, to_all(): return lax.all_to_all(copies, axes, 0, 0, tiled=True)  18.1 us
    ppermute x3, starting transfers between devices, ring_gather(): above.append(lax.ppermute(above[-1], 'z', down))  15.8 us
    ppermute x3, waiting for transfers between devices, ring_gather(): below.append(lax.ppermute(below[-1], 'z', up))  13.1 us
    all_gather x1, waiting for transfers between devices, per_device(): lax.all_gather(jnp.stack([gate_weight, up_weight, probe_gate, probe_up]),...  8.18 us
    pallas_call x1, Pallas kernels, forward(): pl.pallas_call(forward_kernel, out_shape=jax.ShapeDtypeStruct((2, rows, u...  6.88 us
  transfers between devices with their start and end apart: 16, of which 12 were waited for; matrix products, arithmetic and copies ran while one was open for 3% of the time, Pallas kernels for 1%

profile of v3, /device:TPU:1, one launch (start us, length us, event | category | flops | bytes accessed | tf_op | source)
XLA Modules:
  0.0 203.2 jit_solution(9745964647418716676)
XLA Ops:
  7.2 1.8 pad_maximum_fusion.1
  9.8 3.9 %collective-permute-start = (bf16[2,40,256]{2,1,0:T(8,128)(2,1)S(1)}, bf16[2,40,256]{2,1,0:T(8,128)(2,1)S(1)}, u32[]{:S(2)}, u32[]{:S(2)}) collective-permute-start(bf16[2,40,256]{2,1,0:T(8,128)(2,1)S(1)} %get-tuple-element.18), channel_id=1, source_target_pairs={{0,32},{32,0},{1,33},{33,1},{2,34},{34,2},{3,35},{35,3},{4,36},{36... | collective-permute-start | bytes 122888 | tf_op jit(solution)/shard_map/ppermute | solution.py:193
  13.8 1.4 collective-permute-done
  15.2 9.3 %collective-permute-start.1 = (bf16[2,40,256]{2,1,0:T(8,128)(2,1)S(1)}, bf16[2,40,256]{2,1,0:T(8,128)(2,1)S(1)}, u32[]{:S(2)}, u32[]{:S(2)}) collective-permute-start(bf16[2,40,256]{2,1,0:T(8,128)(2,1)S(1)} %get-tuple-element.17), channel_id=1, source_target_pairs={{0,16},{16,0},{1,17},{17,1},{2,18},{18,2},{3,19},{19,3},{4,20},{20... | collective-permute-start | bytes 122888 | tf_op jit(solution)/shard_map/ppermute | solution.py:193
  26.3 1.9 collective-permute-start.2
  28.2 8.8 %collective-permute-done.2 = bf16[352,256]{1,0:T(8,128)(2,1)S(1)} collective-permute-done((bf16[352,256]{1,0:T(8,128)(2,1)S(1)}, bf16[352,256]{1,0:T(8,128)(2,1)S(1)}, u32[]{:S(2)}, u32[]{:S(2)}) %collective-permute-start.2) | collective-permute-done | bytes 180256 | tf_op jit(solution)/shard_map/ppermute | solution.py:193
  38.1 1.9 collective-permute-start.6
  40.0 6.7 %collective-permute-start.3 = (bf16[2,352,256]{2,1,0:T(8,128)(2,1)S(1)}, bf16[2,352,256]{2,1,0:T(8,128)(2,1)}, u32[]{:S(2)}, u32[]{:S(2)}) collective-permute-start(bf16[2,352,256]{2,1,0:T(8,128)(2,1)S(1)} %pad_maximum_fusion), channel_id=1, source_target_pairs={{1,0},{2,1},{3,2},{4,3},{5,4},{6,5},{7,6},{0,7},{9,8},{10,9},{11,1... | collective-permute-start | bytes 1081352 | tf_op jit(solution)/shard_map/ppermute | solution.py:221
  46.7 5.5 %collective-permute-done.6 = bf16[2,352,256]{2,1,0:T(8,128)(2,1)} collective-permute-done((bf16[2,352,256]{2,1,0:T(8,128)(2,1)S(1)}, bf16[2,352,256]{2,1,0:T(8,128)(2,1)}, u32[]{:S(2)}, u32[]{:S(2)}) %collective-permute-start.6) | collective-permute-done | bytes 360480 | tf_op jit(solution)/shard_map/ppermute | solution.py:220
  52.2 1.9 collective-permute-start.7
  54.1 4.6 %collective-permute-start.4 = (bf16[2,352,256]{2,1,0:T(8,128)(2,1)}, bf16[2,352,256]{2,1,0:T(8,128)(2,1)S(1)}, u32[]{:S(2)}, u32[]{:S(2)}) collective-permute-start(bf16[2,352,256]{2,1,0:T(8,128)(2,1)} %collective-permute-done.3), channel_id=1, source_target_pairs={{1,0},{2,1},{3,2},{4,3},{5,4},{6,5},{7,6},{0,7},{9,8},{10,9},{11,1... | collective-permute-start | bytes 1081352 | tf_op jit(solution)/shard_map/ppermute | solution.py:221
  58.8 4.8 %collective-permute-done.7 = bf16[2,352,256]{2,1,0:T(8,128)(2,1)} collective-permute-done((bf16[2,352,256]{2,1,0:T(8,128)(2,1)}, bf16[2,352,256]{2,1,0:T(8,128)(2,1)}, u32[]{:S(2)}, u32[]{:S(2)}) %collective-permute-start.7) | collective-permute-done | bytes 360480 | tf_op jit(solution)/shard_map/ppermute | solution.py:220
  63.5 1.9 collective-permute-start.8
  66.5 4.6 %collective-permute-start.5 = (bf16[2,352,256]{2,1,0:T(8,128)(2,1)S(1)}, bf16[2,352,256]{2,1,0:T(8,128)(2,1)S(1)}, u32[]{:S(2)}, u32[]{:S(2)}) collective-permute-start(bf16[2,352,256]{2,1,0:T(8,128)(2,1)S(1)} %collective-permute-done.4), channel_id=1, source_target_pairs={{1,0},{2,1},{3,2},{4,3},{5,4},{6,5},{7,6},{0,7},{9,8},{10,9},{11,1... | collective-permute-start | bytes 1081352 | tf_op jit(solution)/shard_map/ppermute | solution.py:221
  71.1 2.7 %collective-permute-done.8 = bf16[2,352,256]{2,1,0:T(8,128)(2,1)S(1)} collective-permute-done((bf16[2,352,256]{2,1,0:T(8,128)(2,1)}, bf16[2,352,256]{2,1,0:T(8,128)(2,1)S(1)}, u32[]{:S(2)}, u32[]{:S(2)}) %collective-permute-start.8) | collective-permute-done | bytes 360480 | tf_op jit(solution)/shard_map/ppermute | solution.py:220
  73.9 1.9 collective-permute-start.9
  75.8 5.1 %collective-permute-start.10 = (bf16[352,256]{1,0:T(8,128)(2,1)S(1)}, bf16[352,256]{1,0:T(8,128)(2,1)S(1)}, u32[]{:S(2)}, u32[]{:S(2)}) collective-permute-start(bf16[352,256]{1,0:T(8,128)(2,1)S(1)} %slice_bitcast_fusion), channel_id=1, source_target_pairs={{1,0},{2,1},{3,2},{4,3},{5,4},{6,5},{7,6},{0,7},{9,8},{10,9},{11,1... | collective-permute-start | bytes 540680 | tf_op jit(solution)/shard_map/ppermute | solution.py:223
  81.3 2.0 collective-permute-done.10
  85.4 8.2 %all-gather.3.cloned.1.call-done = bf16[128,80,432]{2,1,0:T(8,128)(2,1)} async-done(((bf16[4,80,432]{2,1,0:T(8,128)(2,1)}), bf16[128,80,432]{2,1,0:T(8,128)(2,1)}) %all-gather.3.cloned.1.call-update) | async-done | bytes 8847376 | tf_op jit(solution)/shard_map/all_gather | solution.py:247
  93.6 6.9 %shard_map.121.refs_0_ = bf16[2,256,432]{2,1,0:T(8,128)(2,1)S(1)} custom-call(s32[1]{0:T(128)} %bitcast.line_ref, bf16[8,2,352,256]{3,2,1,0:T(8,128)(2,1)} %copy-done, bf16[32,4,80,432]{3,2,1,0:T(8,128)(2,1)} %bitcast.56), custom_call_target="tpu_custom_call" | custom-call | flops 2264924160 | bytes 10158080 | tf_op jit(solution)/shard_map/pallas_call | solution.py:64
  100.5 2.8 %collective-permute-start.11 = (bf16[2,256,432]{2,1,0:T(8,128)(2,1)S(1)}, bf16[2,256,432]{2,1,0:T(8,128)(2,1)S(1)}, u32[]{:S(2)}, u32[]{:S(2)}) collective-permute-start(bf16[2,256,432]{2,1,0:T(8,128)(2,1)S(1)} %shard_map.121.refs_0_), channel_id=1, source_target_pairs={{0,32},{32,0},{1,33},{33,1},{2,34},{34,2},{3,35},{35,3},{4,36},{36... | collective-permute-start | bytes 1327112 | tf_op jit(solution)/shard_map/ppermute | solution.py:193
  103.3 2.5 %collective-permute-start.12 = (bf16[2,256,432]{2,1,0:T(8,128)(2,1)S(1)}, bf16[2,256,432]{2,1,0:T(8,128)(2,1)S(1)}, u32[]{:S(2)}, u32[]{:S(2)}) collective-permute-start(bf16[2,256,432]{2,1,0:T(8,128)(2,1)S(1)} %shard_map.121.refs_0_), channel_id=1, source_target_pairs={{0,16},{16,0},{1,17},{17,1},{2,18},{18,2},{3,19},{19,3},{4,20},{20... | collective-permute-start | bytes 1327112 | tf_op jit(solution)/shard_map/ppermute | solution.py:193
  105.8 9.9 %collective-permute-done.11.refs_1_ = bf16[2,256,432]{2,1,0:T(8,128)(2,1)S(1)} collective-permute-done((bf16[2,256,432]{2,1,0:T(8,128)(2,1)S(1)}, bf16[2,256,432]{2,1,0:T(8,128)(2,1)S(1)}, u32[]{:S(2)}, u32[]{:S(2)}) %collective-permute-start.11) | collective-permute-done | bytes 442400 | tf_op jit(solution)/shard_map/ppermute | solution.py:193
  115.7 3.0 %collective-permute-start.13 = (bf16[2,256,432]{2,1,0:T(8,128)(2,1)S(1)}, bf16[2,256,432]{2,1,0:T(8,128)(2,1)S(1)}, u32[]{:S(2)}, u32[]{:S(2)}) collective-permute-start(bf16[2,256,432]{2,1,0:T(8,128)(2,1)S(1)} %collective-permute-done.11.refs_1_), channel_id=1, source_target_pairs={{0,16},{16,0},{1,17},{17,1},{2,18},{18,2},{3,19},{19,3},{4,20},{20... | collective-permute-start | bytes 1327112 | tf_op jit(solution)/shard_map/ppermute | solution.py:193
  118.7 1.5 collective-permute-done.13.refs_3_
  120.2 1.8 copy-done.1
  122.0 3.6 %shard_map.122 = bf16[16,40,866]{2,1,0:T(8,128)(2,1)S(1)} custom-call(s32[1]{0:T(128)} %bitcast.line_ref, bf16[8,2,352,256]{3,2,1,0:T(8,128)(2,1)S(1)} %copy-done.1, bf16[2,256,432]{2,1,0:T(8,128)(2,1)S(1)} %shard_map.121.refs_0_, bf16[2,256,432]{2,1,0:T(8,128)(2,1)S(1)} %collective-permute-done.11.refs_1_, ...), custom_call_target="tpu_custom_call" | custom-call | flops 1358954496 | bytes 5758976 | tf_op jit(solution)/shard_map/pallas_call | solution.py:129
  125.6 35.3 %all_to_all.15.packed_ref = bf16[16,40,866]{2,1,0:T(8,128)(2,1)S(1)} all-to-all(bf16[16,40,866]{2,1,0:T(8,128)(2,1)S(1)} %shard_map.122), channel_id=1, replica_groups=mesh['y'=8,'xl'=2,'core'=2,'xh'=2,'z'=8] {'y','xl'}, dimensions={0} | all-to-all | bytes 2216960 | tf_op jit(solution)/shard_map/all_to_all | solution.py:263
  161.9 18.1 %all_to_all.16 = f32[16,1,128]{2,1,0:T(1,128)S(1)} all-to-all(f32[16,1,128]{2,1,0:T(1,128)S(1)} %broadcast_in_dim.7), channel_id=1, replica_groups=mesh['y'=8,'xl'=2,'core'=2,'xh'=2,'z'=8] {'xh','z'}, dimensions={0} | all-to-all | bytes 16384 | tf_op jit(solution)/shard_map/all_to_all | solution.py:205
  180.7 6.8 %all-to-all-start.2 = ((f32[32,1,128]{2,1,0:T(1,128)}), f32[32,1,128]{2,1,0:T(1,128)S(1)}, u32[]{:S(2)}, u32[]{:S(2)}) async-start(f32[32,1,128]{2,1,0:T(1,128)} %broadcast_in_dim.16), calls=%async_computation.2 | async-start | bytes 32768 | tf_op jit(solution)/shard_map/all_to_all | solution.py:205
  188.2 2.8 %shard_map.124 = f32[80,432]{1,0:T(8,128)S(1)} custom-call(bf16[16,40,866]{2,1,0:T(8,128)(2,1)S(1)} %all_to_all.15.packed_ref), custom_call_target="tpu_custom_call" | custom-call | tf_op jit(solution)/shard_map/pallas_call | solution.py:185
  191.0 4.4 %all-to-all-done.2 = f32[32,1,128]{2,1,0:T(1,128)S(1)} async-done(((f32[32,1,128]{2,1,0:T(1,128)}), f32[32,1,128]{2,1,0:T(1,128)S(1)}, u32[]{:S(2)}, u32[]{:S(2)}) %all-to-all-start.2) | async-done | bytes 16416 | tf_op jit(solution)/shard_map/all_to_all | solution.py:205
  (39 shorter events, 9.6 us)
Async XLA Ops:
  7.2 86.5 %all-gather.3.cloned.1.call-start = ((), (), s32[]{:S(2)}) async-start(), calls=%async_computation.3 | async-start | bytes 10813440 | tf_op jit(solution)/shard_map/all_gather | solution.py:247
  9.8 5.3 %collective-permute-start = (bf16[2,40,256]{2,1,0:T(8,128)(2,1)S(1)}, bf16[2,40,256]{2,1,0:T(8,128)(2,1)S(1)}, u32[]{:S(2)}, u32[]{:S(2)}) collective-permute-start(bf16[2,40,256]{2,1,0:T(8,128)(2,1)S(1)} %get-tuple-element.18), channel_id=1, source_target_pairs={{0,32},{32,0},{1,33},{33,1},{2,34},{34,2},{3,35},{35,3},{4,36},{36... | collective-permute-start | bytes 122888 | tf_op jit(solution)/shard_map/ppermute | solution.py:193
  15.2 10.2 %collective-permute-start.1 = (bf16[2,40,256]{2,1,0:T(8,128)(2,1)S(1)}, bf16[2,40,256]{2,1,0:T(8,128)(2,1)S(1)}, u32[]{:S(2)}, u32[]{:S(2)}) collective-permute-start(bf16[2,40,256]{2,1,0:T(8,128)(2,1)S(1)} %get-tuple-element.17), channel_id=1, source_target_pairs={{0,16},{16,0},{1,17},{17,1},{2,18},{18,2},{3,19},{19,3},{4,20},{20... | collective-permute-start | bytes 122888 | tf_op jit(solution)/shard_map/ppermute | solution.py:193
  26.3 10.8 %collective-permute-start.2 = (bf16[352,256]{1,0:T(8,128)(2,1)S(1)}, bf16[352,256]{1,0:T(8,128)(2,1)S(1)}, u32[]{:S(2)}, u32[]{:S(2)}) collective-permute-start(bf16[352,256]{1,0:T(8,128)(2,1)S(1)} %pad_maximum_fusion.2), channel_id=1, source_target_pairs={{0,8},{8,0},{1,9},{9,1},{2,10},{10,2},{3,11},{11,3},{4,12},{12,4},... | collective-permute-start | bytes 540680 | tf_op jit(solution)/shard_map/ppermute | solution.py:193
  38.1 14.2 %collective-permute-start.6 = (bf16[2,352,256]{2,1,0:T(8,128)(2,1)S(1)}, bf16[2,352,256]{2,1,0:T(8,128)(2,1)}, u32[]{:S(2)}, u32[]{:S(2)}) collective-permute-start(bf16[2,352,256]{2,1,0:T(8,128)(2,1)S(1)} %pad_maximum_fusion), channel_id=1, source_target_pairs={{0,1},{1,2},{2,3},{3,4},{4,5},{5,6},{6,7},{7,0},{8,9},{9,10},{10,1... | collective-permute-start | bytes 1081352 | tf_op jit(solution)/shard_map/ppermute | solution.py:220
  40.0 14.1 %collective-permute-start.3 = (bf16[2,352,256]{2,1,0:T(8,128)(2,1)S(1)}, bf16[2,352,256]{2,1,0:T(8,128)(2,1)}, u32[]{:S(2)}, u32[]{:S(2)}) collective-permute-start(bf16[2,352,256]{2,1,0:T(8,128)(2,1)S(1)} %pad_maximum_fusion), channel_id=1, source_target_pairs={{1,0},{2,1},{3,2},{4,3},{5,4},{6,5},{7,6},{0,7},{9,8},{10,9},{11,1... | collective-permute-start | bytes 1081352 | tf_op jit(solution)/shard_map/ppermute | solution.py:221
  52.2 11.3 %collective-permute-start.7 = (bf16[2,352,256]{2,1,0:T(8,128)(2,1)}, bf16[2,352,256]{2,1,0:T(8,128)(2,1)}, u32[]{:S(2)}, u32[]{:S(2)}) collective-permute-start(bf16[2,352,256]{2,1,0:T(8,128)(2,1)} %collective-permute-done.6), channel_id=1, source_target_pairs={{0,1},{1,2},{2,3},{3,4},{4,5},{5,6},{6,7},{7,0},{8,9},{9,10},{10,1... | collective-permute-start | bytes 1081352 | tf_op jit(solution)/shard_map/ppermute | solution.py:220
  54.1 12.3 %collective-permute-start.4 = (bf16[2,352,256]{2,1,0:T(8,128)(2,1)}, bf16[2,352,256]{2,1,0:T(8,128)(2,1)S(1)}, u32[]{:S(2)}, u32[]{:S(2)}) collective-permute-start(bf16[2,352,256]{2,1,0:T(8,128)(2,1)} %collective-permute-done.3), channel_id=1, source_target_pairs={{1,0},{2,1},{3,2},{4,3},{5,4},{6,5},{7,6},{0,7},{9,8},{10,9},{11,1... | collective-permute-start | bytes 1081352 | tf_op jit(solution)/shard_map/ppermute | solution.py:221
  63.5 10.3 %collective-permute-start.8 = (bf16[2,352,256]{2,1,0:T(8,128)(2,1)}, bf16[2,352,256]{2,1,0:T(8,128)(2,1)S(1)}, u32[]{:S(2)}, u32[]{:S(2)}) collective-permute-start(bf16[2,352,256]{2,1,0:T(8,128)(2,1)} %collective-permute-done.7), channel_id=1, source_target_pairs={{0,1},{1,2},{2,3},{3,4},{4,5},{5,6},{6,7},{7,0},{8,9},{9,10},{10,1... | collective-permute-start | bytes 1081352 | tf_op jit(solution)/shard_map/ppermute | solution.py:220
  66.5 9.3 %collective-permute-start.5 = (bf16[2,352,256]{2,1,0:T(8,128)(2,1)S(1)}, bf16[2,352,256]{2,1,0:T(8,128)(2,1)S(1)}, u32[]{:S(2)}, u32[]{:S(2)}) collective-permute-start(bf16[2,352,256]{2,1,0:T(8,128)(2,1)S(1)} %collective-permute-done.4), channel_id=1, source_target_pairs={{1,0},{2,1},{3,2},{4,3},{5,4},{6,5},{7,6},{0,7},{9,8},{10,9},{11,1... | collective-permute-start | bytes 1081352 | tf_op jit(solution)/shard_map/ppermute | solution.py:221
  73.9 7.4 %collective-permute-start.9 = (bf16[352,256]{1,0:T(8,128)(2,1)S(1)}, bf16[352,256]{1,0:T(8,128)(2,1)S(1)}, u32[]{:S(2)}, u32[]{:S(2)}) collective-permute-start(bf16[352,256]{1,0:T(8,128)(2,1)S(1)} %slice_bitcast_fusion.1), channel_id=1, source_target_pairs={{0,1},{1,2},{2,3},{3,4},{4,5},{5,6},{6,7},{7,0},{8,9},{9,10},{10,1... | collective-permute-start | bytes 540680 | tf_op jit(solution)/shard_map/ppermute | solution.py:222
  75.8 7.5 %collective-permute-start.10 = (bf16[352,256]{1,0:T(8,128)(2,1)S(1)}, bf16[352,256]{1,0:T(8,128)(2,1)S(1)}, u32[]{:S(2)}, u32[]{:S(2)}) collective-permute-start(bf16[352,256]{1,0:T(8,128)(2,1)S(1)} %slice_bitcast_fusion), channel_id=1, source_target_pairs={{1,0},{2,1},{3,2},{4,3},{5,4},{6,5},{7,6},{0,7},{9,8},{10,9},{11,1... | collective-permute-start | bytes 540680 | tf_op jit(solution)/shard_map/ppermute | solution.py:223
  85.4 8.2 %copy-start = (bf16[8,2,352,256]{3,2,1,0:T(8,128)(2,1)}, bf16[8,2,352,256]{3,2,1,0:T(8,128)(2,1)S(1)}, u32[]{:S(2)}) copy-start(bf16[8,2,352,256]{3,2,1,0:T(8,128)(2,1)S(1)} %bitcast_dynamic-update-slice_fusion.feat_ref) | copy-start | bytes 8650756
  100.5 15.1 %collective-permute-start.11 = (bf16[2,256,432]{2,1,0:T(8,128)(2,1)S(1)}, bf16[2,256,432]{2,1,0:T(8,128)(2,1)S(1)}, u32[]{:S(2)}, u32[]{:S(2)}) collective-permute-start(bf16[2,256,432]{2,1,0:T(8,128)(2,1)S(1)} %shard_map.121.refs_0_), channel_id=1, source_target_pairs={{0,32},{32,0},{1,33},{33,1},{2,34},{34,2},{3,35},{35,3},{4,36},{36... | collective-permute-start | bytes 1327112 | tf_op jit(solution)/shard_map/ppermute | solution.py:193
  103.3 15.4 %collective-permute-start.12 = (bf16[2,256,432]{2,1,0:T(8,128)(2,1)S(1)}, bf16[2,256,432]{2,1,0:T(8,128)(2,1)S(1)}, u32[]{:S(2)}, u32[]{:S(2)}) collective-permute-start(bf16[2,256,432]{2,1,0:T(8,128)(2,1)S(1)} %shard_map.121.refs_0_), channel_id=1, source_target_pairs={{0,16},{16,0},{1,17},{17,1},{2,18},{18,2},{3,19},{19,3},{4,20},{20... | collective-permute-start | bytes 1327112 | tf_op jit(solution)/shard_map/ppermute | solution.py:193
  115.7 4.5 %collective-permute-start.13 = (bf16[2,256,432]{2,1,0:T(8,128)(2,1)S(1)}, bf16[2,256,432]{2,1,0:T(8,128)(2,1)S(1)}, u32[]{:S(2)}, u32[]{:S(2)}) collective-permute-start(bf16[2,256,432]{2,1,0:T(8,128)(2,1)S(1)} %collective-permute-done.11.refs_1_), channel_id=1, source_target_pairs={{0,16},{16,0},{1,17},{17,1},{2,18},{18,2},{3,19},{19,3},{4,20},{20... | collective-permute-start | bytes 1327112 | tf_op jit(solution)/shard_map/ppermute | solution.py:193
  120.2 1.8 copy-start.1
  125.6 69.9 %copy-start.2 = (f32[80,432]{1,0:T(8,128)S(1)}, f32[80,432]{1,0:T(8,128)}, u32[]{:S(2)}) copy-start(f32[80,432]{1,0:T(8,128)} %param.18) | copy-start | bytes 414724
  125.6 69.9 %copy-start.3 = (f32[80,432]{1,0:T(8,128)S(1)}, f32[80,432]{1,0:T(8,128)}, u32[]{:S(2)}) copy-start(f32[80,432]{1,0:T(8,128)} %param.17) | copy-start | bytes 414724
  125.6 69.9 %copy-start.4 = (bf16[80,432]{1,0:T(8,128)(2,1)S(1)}, bf16[80,432]{1,0:T(8,128)(2,1)}, u32[]{:S(2)}) copy-start(bf16[80,432]{1,0:T(8,128)(2,1)} %param.16) | copy-start | bytes 207364
  180.7 14.7 %all-to-all-start.2 = ((f32[32,1,128]{2,1,0:T(1,128)}), f32[32,1,128]{2,1,0:T(1,128)S(1)}, u32[]{:S(2)}, u32[]{:S(2)}) async-start(f32[32,1,128]{2,1,0:T(1,128)} %broadcast_in_dim.16), calls=%async_computation.2 | async-start | bytes 32768 | tf_op jit(solution)/shard_map/all_to_all | solution.py:205
Sparse Core Ops, SparseCore 0:
  10.1 83.4 all-gather.2

commit v4 on v3

--- a/solution.py
+++ b/solution.py
@@ -53,8 +53,8 @@
     sigmoid_val = jax.nn.sigmoid(gate_pre)
     silu_val = gate_pre * sigmoid_val
     silu_slope = sigmoid_val * (1.0 + gate_pre * (1.0 - sigmoid_val))
-    out_ref[0] = (silu_val * up_pre).astype(jnp.bfloat16)
-    out_ref[1] = (silu_slope * up_pre * gate_dot + silu_val * up_dot).astype(jnp.bfloat16)
+    out_ref[0] = (silu_val * up_pre).astype(jnp.bfloat16).T
+    out_ref[1] = (silu_slope * up_pre * gate_dot + silu_val * up_dot).astype(jnp.bfloat16).T
 
 
 def forward(line, features, weights):
@@ -63,7 +63,7 @@
     inputs = shards * depth
     return pl.pallas_call(
         forward_kernel,
-        out_shape=jax.ShapeDtypeStruct((2, rows, units), jnp.bfloat16),
+        out_shape=jax.ShapeDtypeStruct((2, units, rows), jnp.bfloat16),
         grid_spec=pltpu.PrefetchScalarGridSpec(
             num_scalar_prefetch=1,
             grid=(pl.cdiv(units, COLUMNS),),
@@ -71,7 +71,7 @@
                 pl.BlockSpec(features.shape, lambda j, line: (0, 0, 0, 0)),
                 pl.BlockSpec((shards, 4, depth, COLUMNS), lambda j, line: (0, 0, 0, j)),
             ],
-            out_specs=pl.BlockSpec((2, rows, COLUMNS), lambda j, line: (0, 0, j)),
+            out_specs=pl.BlockSpec((2, COLUMNS, rows), lambda j, line: (0, j, 0)),
             scratch_shapes=[pltpu.VMEM((rows, inputs), jnp.bfloat16)],
         ),
         compiler_params=pltpu.CompilerParams(vmem_limit_bytes=FORWARD_VMEM),
@@ -94,6 +94,12 @@
     high = block.astype(jnp.bfloat16).astype(jnp.float32)
     rest = jnp.where(top_column(high), block - high, 0.0)
     return high, jnp.sum(rest, axis=1, keepdims=True)
+
+
+def against_rows(left, right):
+    return lax.dot_general(
+        left, right, (((1,), (1,)), ((), ())), preferred_element_type=jnp.float32
+    )
 
 
 def backward_kernel(line_ref, feat_ref, *refs):
@@ -108,7 +114,7 @@
         for index, ref in enumerate(groups):
             begin = start + index * PADDED
             cot = jnp.concatenate([piece[begin : begin + PADDED] for piece in pieces], axis=0)
-            partial = jnp.dot(cot, ref[kind], preferred_element_type=jnp.float32) * (1.0 / TOKENS)
+            partial = against_rows(cot, ref[kind]) * (1.0 / TOKENS)
             total += partial.astype(jnp.bfloat16).astype(jnp.float32)
         return total
 
@@ -123,7 +129,7 @@
 
 def backward(line, features, groups, depth):
     lines, planes, width, rows = features.shape
-    units = groups[0].shape[2]
+    units = groups[0].shape[1]
     shards = lines * planes
     hidden_spec = pl.BlockSpec(groups[0].shape, lambda i, line: (0, 0, 0))
     return pl.pallas_call(

time: 204 us -> 202 us (level)
  no operation moved by 1% of the time
where the time goes in v4:
time: 202 us
  starting transfers between devices  58.8 us (29%)
  blocking collectives  53.4 us (26%)
  waiting for transfers between devices  48.6 us (24%)
  between operations  15.2 us (8%)
  Pallas kernels  14.5 us (7%)
  local copies, waits for them, and re-layouts  6.44 us (3%)
  other arithmetic  4.55 us (2%)
    all_to_all x1, blocking collectives, per_device(): packed = lax.all_to_all(packed, CHIPS, 0, 0, tiled=True)  35.3 us
    ppermute x6, starting transfers between devices, swap(): return lax.ppermute(value, axis, [(0, 1), (1, 0)])  23.4 us
    ppermute x6, waiting for transfers between devices, swap(): return lax.ppermute(value, axis, [(0, 1), (1, 0)])  20.6 us
    all_to_all x1, blocking collectives, to_all(): return lax.all_to_all(copies, axes, 0, 0, tiled=True)  18.1 us
    ppermute x3, starting transfers between devices, ring_gather(): above.append(lax.ppermute(above[-1], 'z', down))  15.8 us
    ppermute x3, waiting for transfers between devices, ring_gather(): below.append(lax.ppermute(below[-1], 'z', up))  13.1 us
    all_gather x1, waiting for transfers between devices, per_device(): lax.all_gather(jnp.stack([gate_weight, up_weight, probe_gate, probe_up]),...  8.18 us
    pallas_call x1, Pallas kernels, forward(): pl.pallas_call(forward_kernel, out_shape=jax.ShapeDtypeStruct((2, units,...  7.13 us
  transfers between devices with their start and end apart: 16, of which 12 were waited for; matrix products, arithmetic and copies ran while one was open for 3% of the time, Pallas kernels for 1%

profile of v4, /device:TPU:1, one launch (start us, length us, event | category | flops | bytes accessed | tf_op | source)
XLA Modules:
  0.0 201.5 jit_solution(3681997553142608807)
XLA Ops:
  7.2 1.8 pad_maximum_fusion.1
  9.8 3.9 %collective-permute-start = (bf16[2,40,256]{2,1,0:T(8,128)(2,1)S(1)}, bf16[2,40,256]{2,1,0:T(8,128)(2,1)S(1)}, u32[]{:S(2)}, u32[]{:S(2)}) collective-permute-start(bf16[2,40,256]{2,1,0:T(8,128)(2,1)S(1)} %get-tuple-element.18), channel_id=1, source_target_pairs={{0,32},{32,0},{1,33},{33,1},{2,34},{34,2},{3,35},{35,3},{4,36},{36... | collective-permute-start | bytes 122888 | tf_op jit(solution)/shard_map/ppermute | solution.py:199
  13.8 1.4 collective-permute-done
  15.2 9.3 %collective-permute-start.1 = (bf16[2,40,256]{2,1,0:T(8,128)(2,1)S(1)}, bf16[2,40,256]{2,1,0:T(8,128)(2,1)S(1)}, u32[]{:S(2)}, u32[]{:S(2)}) collective-permute-start(bf16[2,40,256]{2,1,0:T(8,128)(2,1)S(1)} %get-tuple-element.17), channel_id=1, source_target_pairs={{0,16},{16,0},{1,17},{17,1},{2,18},{18,2},{3,19},{19,3},{4,20},{20... | collective-permute-start | bytes 122888 | tf_op jit(solution)/shard_map/ppermute | solution.py:199
  26.3 1.9 collective-permute-start.2
  28.2 8.8 %collective-permute-done.2 = bf16[352,256]{1,0:T(8,128)(2,1)S(1)} collective-permute-done((bf16[352,256]{1,0:T(8,128)(2,1)S(1)}, bf16[352,256]{1,0:T(8,128)(2,1)S(1)}, u32[]{:S(2)}, u32[]{:S(2)}) %collective-permute-start.2) | collective-permute-done | bytes 180256 | tf_op jit(solution)/shard_map/ppermute | solution.py:199
  38.1 1.9 collective-permute-start.6
  40.0 6.7 %collective-permute-start.3 = (bf16[2,352,256]{2,1,0:T(8,128)(2,1)S(1)}, bf16[2,352,256]{2,1,0:T(8,128)(2,1)}, u32[]{:S(2)}, u32[]{:S(2)}) collective-permute-start(bf16[2,352,256]{2,1,0:T(8,128)(2,1)S(1)} %pad_maximum_fusion), channel_id=1, source_target_pairs={{1,0},{2,1},{3,2},{4,3},{5,4},{6,5},{7,6},{0,7},{9,8},{10,9},{11,1... | collective-permute-start | bytes 1081352 | tf_op jit(solution)/shard_map/ppermute | solution.py:227
  46.7 5.5 %collective-permute-done.6 = bf16[2,352,256]{2,1,0:T(8,128)(2,1)} collective-permute-done((bf16[2,352,256]{2,1,0:T(8,128)(2,1)S(1)}, bf16[2,352,256]{2,1,0:T(8,128)(2,1)}, u32[]{:S(2)}, u32[]{:S(2)}) %collective-permute-start.6) | collective-permute-done | bytes 360480 | tf_op jit(solution)/shard_map/ppermute | solution.py:226
  52.2 1.9 collective-permute-start.7
  54.1 4.6 %collective-permute-start.4 = (bf16[2,352,256]{2,1,0:T(8,128)(2,1)}, bf16[2,352,256]{2,1,0:T(8,128)(2,1)S(1)}, u32[]{:S(2)}, u32[]{:S(2)}) collective-permute-start(bf16[2,352,256]{2,1,0:T(8,128)(2,1)} %collective-permute-done.3), channel_id=1, source_target_pairs={{1,0},{2,1},{3,2},{4,3},{5,4},{6,5},{7,6},{0,7},{9,8},{10,9},{11,1... | collective-permute-start | bytes 1081352 | tf_op jit(solution)/shard_map/ppermute | solution.py:227
  58.8 4.8 %collective-permute-done.7 = bf16[2,352,256]{2,1,0:T(8,128)(2,1)} collective-permute-done((bf16[2,352,256]{2,1,0:T(8,128)(2,1)}, bf16[2,352,256]{2,1,0:T(8,128)(2,1)}, u32[]{:S(2)}, u32[]{:S(2)}) %collective-permute-start.7) | collective-permute-done | bytes 360480 | tf_op jit(solution)/shard_map/ppermute | solution.py:226
  63.5 1.9 collective-permute-start.8
  66.5 4.6 %collective-permute-start.5 = (bf16[2,352,256]{2,1,0:T(8,128)(2,1)S(1)}, bf16[2,352,256]{2,1,0:T(8,128)(2,1)S(1)}, u32[]{:S(2)}, u32[]{:S(2)}) collective-permute-start(bf16[2,352,256]{2,1,0:T(8,128)(2,1)S(1)} %collective-permute-done.4), channel_id=1, source_target_pairs={{1,0},{2,1},{3,2},{4,3},{5,4},{6,5},{7,6},{0,7},{9,8},{10,9},{11,1... | collective-permute-start | bytes 1081352 | tf_op jit(solution)/shard_map/ppermute | solution.py:227
  71.1 2.7 %collective-permute-done.8 = bf16[2,352,256]{2,1,0:T(8,128)(2,1)S(1)} collective-permute-done((bf16[2,352,256]{2,1,0:T(8,128)(2,1)}, bf16[2,352,256]{2,1,0:T(8,128)(2,1)S(1)}, u32[]{:S(2)}, u32[]{:S(2)}) %collective-permute-start.8) | collective-permute-done | bytes 360480 | tf_op jit(solution)/shard_map/ppermute | solution.py:226
  73.9 1.9 collective-permute-start.9
  75.8 5.1 %collective-permute-start.10 = (bf16[352,256]{1,0:T(8,128)(2,1)S(1)}, bf16[352,256]{1,0:T(8,128)(2,1)S(1)}, u32[]{:S(2)}, u32[]{:S(2)}) collective-permute-start(bf16[352,256]{1,0:T(8,128)(2,1)S(1)} %slice_bitcast_fusion), channel_id=1, source_target_pairs={{1,0},{2,1},{3,2},{4,3},{5,4},{6,5},{7,6},{0,7},{9,8},{10,9},{11,1... | collective-permute-start | bytes 540680 | tf_op jit(solution)/shard_map/ppermute | solution.py:229
  81.3 2.0 collective-permute-done.10
  85.4 8.2 %all-gather.3.cloned.1.call-done = bf16[128,80,432]{2,1,0:T(8,128)(2,1)} async-done(((bf16[4,80,432]{2,1,0:T(8,128)(2,1)}), bf16[128,80,432]{2,1,0:T(8,128)(2,1)}) %all-gather.3.cloned.1.call-update) | async-done | bytes 8847376 | tf_op jit(solution)/shard_map/all_gather | solution.py:253
  93.6 7.1 %shard_map.121.refs_0_ = bf16[2,432,256]{2,1,0:T(8,128)(2,1)S(1)} custom-call(s32[1]{0:T(128)} %bitcast.line_ref, bf16[8,2,352,256]{3,2,1,0:T(8,128)(2,1)} %copy-done, bf16[32,4,80,432]{3,2,1,0:T(8,128)(2,1)} %bitcast.56), custom_call_target="tpu_custom_call" | custom-call | flops 2264924160 | bytes 10158080 | tf_op jit(solution)/shard_map/pallas_call | solution.py:64
  100.8 2.8 %collective-permute-start.11 = (bf16[2,432,256]{2,1,0:T(8,128)(2,1)S(1)}, bf16[2,432,256]{2,1,0:T(8,128)(2,1)S(1)}, u32[]{:S(2)}, u32[]{:S(2)}) collective-permute-start(bf16[2,432,256]{2,1,0:T(8,128)(2,1)S(1)} %shard_map.121.refs_0_), channel_id=1, source_target_pairs={{0,32},{32,0},{1,33},{33,1},{2,34},{34,2},{3,35},{35,3},{4,36},{36... | collective-permute-start | bytes 1327112 | tf_op jit(solution)/shard_map/ppermute | solution.py:199
  103.6 2.5 %collective-permute-start.12 = (bf16[2,432,256]{2,1,0:T(8,128)(2,1)S(1)}, bf16[2,432,256]{2,1,0:T(8,128)(2,1)S(1)}, u32[]{:S(2)}, u32[]{:S(2)}) collective-permute-start(bf16[2,432,256]{2,1,0:T(8,128)(2,1)S(1)} %shard_map.121.refs_0_), channel_id=1, source_target_pairs={{0,16},{16,0},{1,17},{17,1},{2,18},{18,2},{3,19},{19,3},{4,20},{20... | collective-permute-start | bytes 1327112 | tf_op jit(solution)/shard_map/ppermute | solution.py:199
  106.0 8.1 %collective-permute-done.11.refs_1_ = bf16[2,432,256]{2,1,0:T(8,128)(2,1)S(1)} collective-permute-done((bf16[2,432,256]{2,1,0:T(8,128)(2,1)S(1)}, bf16[2,432,256]{2,1,0:T(8,128)(2,1)S(1)}, u32[]{:S(2)}, u32[]{:S(2)}) %collective-permute-start.11) | collective-permute-done | bytes 442400 | tf_op jit(solution)/shard_map/ppermute | solution.py:199
  114.2 3.0 %collective-permute-start.13 = (bf16[2,432,256]{2,1,0:T(8,128)(2,1)S(1)}, bf16[2,432,256]{2,1,0:T(8,128)(2,1)S(1)}, u32[]{:S(2)}, u32[]{:S(2)}) collective-permute-start(bf16[2,432,256]{2,1,0:T(8,128)(2,1)S(1)} %collective-permute-done.11.refs_1_), channel_id=1, source_target_pairs={{0,16},{16,0},{1,17},{17,1},{2,18},{18,2},{3,19},{19,3},{4,20},{20... | collective-permute-start | bytes 1327112 | tf_op jit(solution)/shard_map/ppermute | solution.py:199
  117.2 1.4 collective-permute-done.13.refs_3_
  118.6 1.8 copy-done.1
  120.4 3.6 %shard_map.122 = bf16[16,40,866]{2,1,0:T(8,128)(2,1)S(1)} custom-call(s32[1]{0:T(128)} %bitcast.line_ref, bf16[8,2,352,256]{3,2,1,0:T(8,128)(2,1)S(1)} %copy-done.1, bf16[2,432,256]{2,1,0:T(8,128)(2,1)S(1)} %shard_map.121.refs_0_, bf16[2,432,256]{2,1,0:T(8,128)(2,1)S(1)} %collective-permute-done.11.refs_1_, ...), custom_call_target="tpu_custom_call" | custom-call | flops 1358954496 | bytes 5758976 | tf_op jit(solution)/shard_map/pallas_call | solution.py:135
  124.0 35.3 %all_to_all.15.packed_ref = bf16[16,40,866]{2,1,0:T(8,128)(2,1)S(1)} all-to-all(bf16[16,40,866]{2,1,0:T(8,128)(2,1)S(1)} %shard_map.122), channel_id=1, replica_groups=mesh['y'=8,'xl'=2,'core'=2,'xh'=2,'z'=8] {'y','xl'}, dimensions={0} | all-to-all | bytes 2216960 | tf_op jit(solution)/shard_map/all_to_all | solution.py:269
  160.3 18.1 %all_to_all.16 = f32[16,1,128]{2,1,0:T(1,128)S(1)} all-to-all(f32[16,1,128]{2,1,0:T(1,128)S(1)} %broadcast_in_dim.7), channel_id=1, replica_groups=mesh['y'=8,'xl'=2,'core'=2,'xh'=2,'z'=8] {'xh','z'}, dimensions={0} | all-to-all | bytes 16384 | tf_op jit(solution)/shard_map/all_to_all | solution.py:211
  179.0 6.8 %all-to-all-start.2 = ((f32[32,1,128]{2,1,0:T(1,128)}), f32[32,1,128]{2,1,0:T(1,128)S(1)}, u32[]{:S(2)}, u32[]{:S(2)}) async-start(f32[32,1,128]{2,1,0:T(1,128)} %broadcast_in_dim.16), calls=%async_computation.2 | async-start | bytes 32768 | tf_op jit(solution)/shard_map/all_to_all | solution.py:211
  186.5 2.8 %shard_map.124 = f32[80,432]{1,0:T(8,128)S(1)} custom-call(bf16[16,40,866]{2,1,0:T(8,128)(2,1)S(1)} %all_to_all.15.packed_ref), custom_call_target="tpu_custom_call" | custom-call | tf_op jit(solution)/shard_map/pallas_call | solution.py:191
  189.4 4.4 %all-to-all-done.2 = f32[32,1,128]{2,1,0:T(1,128)S(1)} async-done(((f32[32,1,128]{2,1,0:T(1,128)}), f32[32,1,128]{2,1,0:T(1,128)S(1)}, u32[]{:S(2)}, u32[]{:S(2)}) %all-to-all-start.2) | async-done | bytes 16416 | tf_op jit(solution)/shard_map/all_to_all | solution.py:211
  (39 shorter events, 9.6 us)
Async XLA Ops:
  7.2 86.5 %all-gather.3.cloned.1.call-start = ((), (), s32[]{:S(2)}) async-start(), calls=%async_computation.3 | async-start | bytes 10813440 | tf_op jit(solution)/shard_map/all_gather | solution.py:253
  9.8 5.3 %collective-permute-start = (bf16[2,40,256]{2,1,0:T(8,128)(2,1)S(1)}, bf16[2,40,256]{2,1,0:T(8,128)(2,1)S(1)}, u32[]{:S(2)}, u32[]{:S(2)}) collective-permute-start(bf16[2,40,256]{2,1,0:T(8,128)(2,1)S(1)} %get-tuple-element.18), channel_id=1, source_target_pairs={{0,32},{32,0},{1,33},{33,1},{2,34},{34,2},{3,35},{35,3},{4,36},{36... | collective-permute-start | bytes 122888 | tf_op jit(solution)/shard_map/ppermute | solution.py:199
  15.2 10.2 %collective-permute-start.1 = (bf16[2,40,256]{2,1,0:T(8,128)(2,1)S(1)}, bf16[2,40,256]{2,1,0:T(8,128)(2,1)S(1)}, u32[]{:S(2)}, u32[]{:S(2)}) collective-permute-start(bf16[2,40,256]{2,1,0:T(8,128)(2,1)S(1)} %get-tuple-element.17), channel_id=1, source_target_pairs={{0,16},{16,0},{1,17},{17,1},{2,18},{18,2},{3,19},{19,3},{4,20},{20... | collective-permute-start | bytes 122888 | tf_op jit(solution)/shard_map/ppermute | solution.py:199
  26.3 10.8 %collective-permute-start.2 = (bf16[352,256]{1,0:T(8,128)(2,1)S(1)}, bf16[352,256]{1,0:T(8,128)(2,1)S(1)}, u32[]{:S(2)}, u32[]{:S(2)}) collective-permute-start(bf16[352,256]{1,0:T(8,128)(2,1)S(1)} %pad_maximum_fusion.2), channel_id=1, source_target_pairs={{0,8},{8,0},{1,9},{9,1},{2,10},{10,2},{3,11},{11,3},{4,12},{12,4},... | collective-permute-start | bytes 540680 | tf_op jit(solution)/shard_map/ppermute | solution.py:199
  38.1 14.2 %collective-permute-start.6 = (bf16[2,352,256]{2,1,0:T(8,128)(2,1)S(1)}, bf16[2,352,256]{2,1,0:T(8,128)(2,1)}, u32[]{:S(2)}, u32[]{:S(2)}) collective-permute-start(bf16[2,352,256]{2,1,0:T(8,128)(2,1)S(1)} %pad_maximum_fusion), channel_id=1, source_target_pairs={{0,1},{1,2},{2,3},{3,4},{4,5},{5,6},{6,7},{7,0},{8,9},{9,10},{10,1... | collective-permute-start | bytes 1081352 | tf_op jit(solution)/shard_map/ppermute | solution.py:226
  40.0 14.1 %collective-permute-start.3 = (bf16[2,352,256]{2,1,0:T(8,128)(2,1)S(1)}, bf16[2,352,256]{2,1,0:T(8,128)(2,1)}, u32[]{:S(2)}, u32[]{:S(2)}) collective-permute-start(bf16[2,352,256]{2,1,0:T(8,128)(2,1)S(1)} %pad_maximum_fusion), channel_id=1, source_target_pairs={{1,0},{2,1},{3,2},{4,3},{5,4},{6,5},{7,6},{0,7},{9,8},{10,9},{11,1... | collective-permute-start | bytes 1081352 | tf_op jit(solution)/shard_map/ppermute | solution.py:227
  52.2 11.3 %collective-permute-start.7 = (bf16[2,352,256]{2,1,0:T(8,128)(2,1)}, bf16[2,352,256]{2,1,0:T(8,128)(2,1)}, u32[]{:S(2)}, u32[]{:S(2)}) collective-permute-start(bf16[2,352,256]{2,1,0:T(8,128)(2,1)} %collective-permute-done.6), channel_id=1, source_target_pairs={{0,1},{1,2},{2,3},{3,4},{4,5},{5,6},{6,7},{7,0},{8,9},{9,10},{10,1... | collective-permute-start | bytes 1081352 | tf_op jit(solution)/shard_map/ppermute | solution.py:226
  54.1 12.3 %collective-permute-start.4 = (bf16[2,352,256]{2,1,0:T(8,128)(2,1)}, bf16[2,352,256]{2,1,0:T(8,128)(2,1)S(1)}, u32[]{:S(2)}, u32[]{:S(2)}) collective-permute-start(bf16[2,352,256]{2,1,0:T(8,128)(2,1)} %collective-permute-done.3), channel_id=1, source_target_pairs={{1,0},{2,1},{3,2},{4,3},{5,4},{6,5},{7,6},{0,7},{9,8},{10,9},{11,1... | collective-permute-start | bytes 1081352 | tf_op jit(solution)/shard_map/ppermute | solution.py:227
  63.5 10.3 %collective-permute-start.8 = (bf16[2,352,256]{2,1,0:T(8,128)(2,1)}, bf16[2,352,256]{2,1,0:T(8,128)(2,1)S(1)}, u32[]{:S(2)}, u32[]{:S(2)}) collective-permute-start(bf16[2,352,256]{2,1,0:T(8,128)(2,1)} %collective-permute-done.7), channel_id=1, source_target_pairs={{0,1},{1,2},{2,3},{3,4},{4,5},{5,6},{6,7},{7,0},{8,9},{9,10},{10,1... | collective-permute-start | bytes 1081352 | tf_op jit(solution)/shard_map/ppermute | solution.py:226
  66.5 9.3 %collective-permute-start.5 = (bf16[2,352,256]{2,1,0:T(8,128)(2,1)S(1)}, bf16[2,352,256]{2,1,0:T(8,128)(2,1)S(1)}, u32[]{:S(2)}, u32[]{:S(2)}) collective-permute-start(bf16[2,352,256]{2,1,0:T(8,128)(2,1)S(1)} %collective-permute-done.4), channel_id=1, source_target_pairs={{1,0},{2,1},{3,2},{4,3},{5,4},{6,5},{7,6},{0,7},{9,8},{10,9},{11,1... | collective-permute-start | bytes 1081352 | tf_op jit(solution)/shard_map/ppermute | solution.py:227
  73.9 7.4 %collective-permute-start.9 = (bf16[352,256]{1,0:T(8,128)(2,1)S(1)}, bf16[352,256]{1,0:T(8,128)(2,1)S(1)}, u32[]{:S(2)}, u32[]{:S(2)}) collective-permute-start(bf16[352,256]{1,0:T(8,128)(2,1)S(1)} %slice_bitcast_fusion.1), channel_id=1, source_target_pairs={{0,1},{1,2},{2,3},{3,4},{4,5},{5,6},{6,7},{7,0},{8,9},{9,10},{10,1... | collective-permute-start | bytes 540680 | tf_op jit(solution)/shard_map/ppermute | solution.py:228
  75.8 7.5 %collective-permute-start.10 = (bf16[352,256]{1,0:T(8,128)(2,1)S(1)}, bf16[352,256]{1,0:T(8,128)(2,1)S(1)}, u32[]{:S(2)}, u32[]{:S(2)}) collective-permute-start(bf16[352,256]{1,0:T(8,128)(2,1)S(1)} %slice_bitcast_fusion), channel_id=1, source_target_pairs={{1,0},{2,1},{3,2},{4,3},{5,4},{6,5},{7,6},{0,7},{9,8},{10,9},{11,1... | collective-permute-start | bytes 540680 | tf_op jit(solution)/shard_map/ppermute | solution.py:229
  85.4 8.2 %copy-start = (bf16[8,2,352,256]{3,2,1,0:T(8,128)(2,1)}, bf16[8,2,352,256]{3,2,1,0:T(8,128)(2,1)S(1)}, u32[]{:S(2)}) copy-start(bf16[8,2,352,256]{3,2,1,0:T(8,128)(2,1)S(1)} %bitcast_dynamic-update-slice_fusion.feat_ref) | copy-start | bytes 8650756
  100.8 13.4 %collective-permute-start.11 = (bf16[2,432,256]{2,1,0:T(8,128)(2,1)S(1)}, bf16[2,432,256]{2,1,0:T(8,128)(2,1)S(1)}, u32[]{:S(2)}, u32[]{:S(2)}) collective-permute-start(bf16[2,432,256]{2,1,0:T(8,128)(2,1)S(1)} %shard_map.121.refs_0_), channel_id=1, source_target_pairs={{0,32},{32,0},{1,33},{33,1},{2,34},{34,2},{3,35},{35,3},{4,36},{36... | collective-permute-start | bytes 1327112 | tf_op jit(solution)/shard_map/ppermute | solution.py:199
  103.6 13.6 %collective-permute-start.12 = (bf16[2,432,256]{2,1,0:T(8,128)(2,1)S(1)}, bf16[2,432,256]{2,1,0:T(8,128)(2,1)S(1)}, u32[]{:S(2)}, u32[]{:S(2)}) collective-permute-start(bf16[2,432,256]{2,1,0:T(8,128)(2,1)S(1)} %shard_map.121.refs_0_), channel_id=1, source_target_pairs={{0,16},{16,0},{1,17},{17,1},{2,18},{18,2},{3,19},{19,3},{4,20},{20... | collective-permute-start | bytes 1327112 | tf_op jit(solution)/shard_map/ppermute | solution.py:199
  114.2 4.4 %collective-permute-start.13 = (bf16[2,432,256]{2,1,0:T(8,128)(2,1)S(1)}, bf16[2,432,256]{2,1,0:T(8,128)(2,1)S(1)}, u32[]{:S(2)}, u32[]{:S(2)}) collective-permute-start(bf16[2,432,256]{2,1,0:T(8,128)(2,1)S(1)} %collective-permute-done.11.refs_1_), channel_id=1, source_target_pairs={{0,16},{16,0},{1,17},{17,1},{2,18},{18,2},{3,19},{19,3},{4,20},{20... | collective-permute-start | bytes 1327112 | tf_op jit(solution)/shard_map/ppermute | solution.py:199
  118.6 1.8 copy-start.1
  123.9 69.9 %copy-start.2 = (f32[80,432]{1,0:T(8,128)S(1)}, f32[80,432]{1,0:T(8,128)}, u32[]{:S(2)}) copy-start(f32[80,432]{1,0:T(8,128)} %param.18) | copy-start | bytes 414724
  123.9 69.9 %copy-start.3 = (f32[80,432]{1,0:T(8,128)S(1)}, f32[80,432]{1,0:T(8,128)}, u32[]{:S(2)}) copy-start(f32[80,432]{1,0:T(8,128)} %param.17) | copy-start | bytes 414724
  124.0 69.9 %copy-start.4 = (bf16[80,432]{1,0:T(8,128)(2,1)S(1)}, bf16[80,432]{1,0:T(8,128)(2,1)}, u32[]{:S(2)}) copy-start(bf16[80,432]{1,0:T(8,128)(2,1)} %param.16) | copy-start | bytes 207364
  179.0 14.7 %all-to-all-start.2 = ((f32[32,1,128]{2,1,0:T(1,128)}), f32[32,1,128]{2,1,0:T(1,128)S(1)}, u32[]{:S(2)}, u32[]{:S(2)}) async-start(f32[32,1,128]{2,1,0:T(1,128)} %broadcast_in_dim.16), calls=%async_computation.2 | async-start | bytes 32768 | tf_op jit(solution)/shard_map/all_to_all | solution.py:211
Sparse Core Ops, SparseCore 0:
  10.1 83.4 all-gather.2
